TPU v7x, 128 devices: a whole 4x4x4 slice. The times are simulated.
128 devices in a mesh: dom: 32 (over x, y, z_hi), smp: 4 (over z_lo, core).
Axes of the slice: x: 4, y: 4, z: 4 (z_hi: 2, z_lo: 2; z = z_hi * 2 + z_lo), core: 2. Of those that a mesh axis runs over, the one named last changes fastest.
Arguments:
- state_before: float32 [4, 256, 128, 256], P('smp', 'dom'), may hold values from -6 to 6
- state_now: float32 [4, 256, 128, 256], P('smp', 'dom'), may hold values from -6 to 6
- base_model: float32 [256, 128, 256], P('dom'), may hold values from 0.06 to 0.16
- buoyancy: float32 [256, 128, 256], P('dom'), may hold values from 0.5 to 1.5
- latent: float32 [4, 256, 128, 256], P('smp', 'dom'), may hold values from -6 to 6
- flow_gain: bfloat16 [256, 128, 256], P('dom', 'smp'), may hold values from -6 to 6
- flow_bias: bfloat16 [256, 128, 256], P('dom', 'smp'), may hold values from -3 to 3
- records: bfloat16 [64, 4, 256, 128], P('dom'), may hold values from -6 to 6
- source_wavelet: float32 [64, 4], replicated, may hold values from -32 to 32
- source_cell: int32 [64], replicated, may hold values from 0 to 8388607
- shot: int32 [1], replicated, may hold values from 0 to 63
- receiver_depth: int32 [256, 128], P('dom'), may hold values from 1 to 254
Outputs:
- image: float32 [4, 256, 128, 256], P('smp', 'dom')
- gain_grad: float32 [256, 128, 256], P('dom', 'smp')
- bias_grad: float32 [256, 128, 256], P('dom', 'smp')
All inputs are finite; a program needn't handle non-finite values.
Results may differ from a plain program's by a relative error of at most 0.0003.
Values may be sent and summed in bfloat16 or wider, within the bound.
A program may use at most 64 MiB of HBM per device.

v0:
```python
import jax
import jax.numpy as jnp
from jax import lax
from jax.sharding import PartitionSpec as P


def spread(shard, axis, root):
    mine = lax.axis_index(axis) == root
    return lax.psum(jnp.where(mine, shard, jnp.zeros_like(shard)), axis)


def with_halo(cells, sides, width):
    for axis, dim in sides:
        count = lax.axis_size(axis)
        ends = count - 1
        head = lax.slice_in_dim(cells, 0, width, axis=dim)
        tail = lax.slice_in_dim(cells, cells.shape[dim] - width, cells.shape[dim], axis=dim)
        cells = jnp.concatenate(
            [
                lax.ppermute(tail, axis, [(i, (i + 1) % count) for i in range(ends)]),
                cells,
                lax.ppermute(head, axis, [((i + 1) % count, i) for i in range(ends)]),
            ],
            axis=dim,
        )
    return cells


def operate_padded(field, buoy):
    middle = field[1:-1]
    middle_buoy = buoy[1:-1]
    total = 0.5 * (middle_buoy + buoy[2:]) * (field[2:] - middle) + 0.5 * (
        middle_buoy + buoy[:-2]
    ) * (field[:-2] - middle)
    side_field = jnp.pad(middle, ((0, 0), (1, 1), (0, 0)))
    side_buoy = jnp.pad(middle_buoy, ((0, 0), (1, 1), (0, 0)))
    total = (
        total
        + 0.5 * (middle_buoy + side_buoy[:, 2:]) * (side_field[:, 2:] - middle)
        + 0.5 * (middle_buoy + side_buoy[:, :-2]) * (side_field[:, :-2] - middle)
    )
    deep_field = jnp.pad(middle, ((0, 0), (0, 0), (1, 1)))
    deep_buoy = jnp.pad(middle_buoy, ((0, 0), (0, 0), (1, 1)))
    total = (
        total
        + 0.5 * (middle_buoy + deep_buoy[:, :, 2:]) * (deep_field[:, :, 2:] - middle)
        + 0.5 * (middle_buoy + deep_buoy[:, :, :-2]) * (deep_field[:, :, :-2] - middle)
    )
    return total


def shards(
    state_before,
    state_now,
    base_model,
    buoyancy,
    latent,
    flow_gain,
    flow_bias,
    records,
    source_wavelet,
    source_cell,
    shot,
    receiver_depth,
):
    slab_width = base_model.shape[0]
    extent_y = base_model.shape[1]
    extent_z = base_model.shape[2]
    steps_count = source_wavelet.shape[1]
    stored_count = records.shape[0]
    picked = shot[0]
    place = lax.axis_index("dom")
    first_row = place * slab_width
    gain_all, bias_all = (
        lax.all_gather(flow_gain, "smp", axis=1, tiled=True),
        lax.all_gather(flow_bias, "smp", axis=1, tiled=True),
    )
    latent_own = latent[0]
    squash = jnp.tanh(latent_own * gain_all.astype(jnp.float32) + bias_all.astype(jnp.float32))
    model = base_model * jnp.exp(0.25 * squash)
    mine = lax.dynamic_index_in_dim(records, picked % stored_count, 0, keepdims=False)
    whole = spread(mine, "dom", picked // stored_count)
    record = lax.dynamic_slice_in_dim(whole, first_row, slab_width, 1).astype(jnp.float32)
    wavelet = lax.dynamic_index_in_dim(source_wavelet, picked, 0, keepdims=False)
    flat_cell = lax.dynamic_index_in_dim(source_cell, picked, 0, keepdims=False)
    cell_x = flat_cell // (extent_y * extent_z)
    cell_y = flat_cell // extent_z % extent_y
    cell_z = flat_cell % extent_z
    rows_y = lax.iota(jnp.int32, extent_y)
    rows_z = lax.iota(jnp.int32, extent_z)
    plane_hit = (rows_y[:, None] == cell_y) & (rows_z[None, :] == cell_z)
    onehot = (rows_z[None, None, :] == receiver_depth[:, :, None]).astype(jnp.float32)
    state_images = []
    residuals = []
    coef_padded = with_halo(buoyancy, (("dom", 0),), 1)
    previous = state_before[0]
    current = state_now[0]
    rows_x = first_row + lax.iota(jnp.int32, slab_width)
    point = ((rows_x[:, None, None] == cell_x) & plane_hit[None, :, :]).astype(jnp.float32)
    for turn in range(steps_count):
        padded = with_halo(current, (("dom", 0),), 1)
        applied = operate_padded(padded, coef_padded)
        state_images.append(applied)
        following = 2.0 * current - previous + model * applied + wavelet[turn] * point
        residuals.append(jnp.sum(following * onehot, axis=2) - record[turn])
        previous = current
        current = following
    later = jnp.zeros(base_model.shape, jnp.float32)
    latest = jnp.zeros(base_model.shape, jnp.float32)
    image = jnp.zeros(base_model.shape, jnp.float32)
    for turn in reversed(range(steps_count)):
        injected = residuals[turn][:, :, None] * onehot
        if turn == steps_count - 1:
            adjoint = 2.0 * later + injected
        else:
            scaled = with_halo(model * later, (("dom", 0),), 1)
            adjoint = 2.0 * later - latest + operate_padded(scaled, coef_padded) + injected
        image = image + adjoint * state_images[turn]
        latest = later
        later = adjoint
    common = image * model * 0.25 * (1.0 - squash * squash)
    gain_grad, bias_grad = (
        lax.psum_scatter(common * latent_own, "smp", scatter_dimension=1, tiled=True),
        lax.psum_scatter(common, "smp", scatter_dimension=1, tiled=True),
    )
    return (image[None], gain_grad, bias_grad)


def solution(mesh):
    in_specs = (
        P("smp", "dom", None, None),
        P("smp", "dom", None, None),
        P("dom", None, None),
        P("dom", None, None),
        P("smp", "dom", None, None),
        P("dom", "smp", None),
        P("dom", "smp", None),
        P("dom", None, None, None),
        P(),
        P(),
        P(),
        P("dom", None),
    )
    out_specs = (P("smp", "dom", None, None), P("dom", "smp", None), P("dom", "smp", None))
    return jax.shard_map(shards, mesh=mesh, in_specs=in_specs, out_specs=out_specs, check_vma=False)
```

profile of v0, /device:TPU:1, one launch (start us, length us, event | category | flops | bytes accessed | tf_op | source)
XLA Modules:
  0.0 554.9 jit_solution(14813718339653198946)
XLA Ops:
  8.3 1.4 collective-permute-start.1
  9.8 7.0 %collective-permute-start.3 = (f32[1,128,256]{2,1,0:T(8,128)S(1)}, f32[1,128,256]{2,1,0:T(8,128)S(1)}, u32[]{:S(2)}, u32[]{:S(2)}) collective-permute-start(f32[1,128,256]{2,1,0:T(8,128)S(1)} %get-tuple-element.38), channel_id=1, source_target_pairs={{0,4},{4,8},{8,12},{12,16},{16,20},{20,24},{24,28},{28,32},{32,36}... | collective-permute-start | bytes 393224 | tf_op jit(solution)/shard_map/ppermute | solution.py:20
  17.7 1.3 collective-permute-start
  19.0 6.4 %collective-permute-start.2 = (f32[1,128,256]{2,1,0:T(8,128)S(1)}, f32[1,128,256]{2,1,0:T(8,128)S(1)}, u32[]{:S(2)}, u32[]{:S(2)}) collective-permute-start(f32[1,128,256]{2,1,0:T(8,128)S(1)} %get-tuple-element.36), channel_id=1, source_target_pairs={{0,4},{4,8},{8,12},{12,16},{16,20},{20,24},{24,28},{28,32},{32,36}... | collective-permute-start | bytes 393224 | tf_op jit(solution)/shard_map/ppermute | solution.py:20
  29.4 8.5 %all_gather.6 = bf16[8,128,256]{2,1,0:T(8,128)(2,1)} all-gather(bf16[8,32,256]{2,1,0:T(8,128)(2,1)S(1)} %copy-done.20), channel_id=1, replica_groups=mesh['dom'=32,'smp'=4] {'smp'}, dimensions={1}, use_global_device_ids=true | all-gather | bytes 655360 | tf_op jit(solution)/shard_map/all_gather | solution.py:75
  37.9 7.7 %all_gather.7 = bf16[8,128,256]{2,1,0:T(8,128)(2,1)} all-gather(bf16[8,32,256]{2,1,0:T(8,128)(2,1)S(1)} %copy-done.21), channel_id=1, replica_groups=mesh['dom'=32,'smp'=4] {'smp'}, dimensions={1}, use_global_device_ids=true | all-gather | bytes 655360 | tf_op jit(solution)/shard_map/all_gather | solution.py:76
  47.1 8.5 %fusion.100 = (f32[8,128,256]{2,1,0:T(8,128)S(1)}, f32[8,128,256]{2,1,0:T(8,128)S(1)}, f32[8,128,256]{2,1,0:T(8,128)}, f32[8,128,256]{2,1,0:T(8,128)S(1)}, f32[8...) fusion(f32[1,8,128,256]{3,2,1,0:T(8,128)} %param.12, f32[]{:T(128)} %bitcast.7, ...), kind=kLoop, calls=%fused_computation.140 | loop fusion | flops 12058624 | bytes 15237132 | tf_op jit(solution)/shard_map/add | solution.py:104
  55.6 1.3 collective-permute-start.4
  56.9 7.3 %collective-permute-start.5 = (f32[1,128,256]{2,1,0:T(8,128)S(1)}, f32[1,128,256]{2,1,0:T(8,128)S(1)}, u32[]{:S(2)}, u32[]{:S(2)}) collective-permute-start(f32[1,128,256]{2,1,0:T(8,128)S(1)} %get-tuple-element.34), channel_id=1, source_target_pairs={{0,4},{4,8},{8,12},{12,16},{16,20},{20,24},{24,28},{28,32},{32,36}... | collective-permute-start | bytes 393224 | tf_op jit(solution)/shard_map/ppermute | solution.py:20
  64.2 1.8 collective-permute-done.4
  66.0 3.2 collective-permute-done.5
  69.2 3.5 fusion.101
  75.7 6.9 %collective-permute-start.7 = (f32[1,128,256]{2,1,0:T(8,128)}, f32[1,128,256]{2,1,0:T(8,128)}, u32[]{:S(2)}, u32[]{:S(2)}) collective-permute-start(f32[1,128,256]{2,1,0:T(8,128)} %get-tuple-element.32), channel_id=1, source_target_pairs={{0,4},{4,8},{8,12},{12,16},{16,20},{20,24},{24,28},{28,32},{32,36}... | collective-permute-start | bytes 393224 | tf_op jit(solution)/shard_map/ppermute | solution.py:20
  82.6 1.7 select_bitcast_fusion
  84.3 2.9 collective-permute-done.7
  87.2 9.5 %select_reduce_fusion = (f32[8,128]{1,0:T(8,128)S(1)}, f32[8,128]{1,0:T(8,128)S(1)}, f32[8,128]{1,0:T(8,128)S(1)}, f32[8,128,256]{2,1,0:T(8,128)S(1)}) fusion(f32[8,128,256]{2,1,0:T(8,128)} %copy-done.9, s32[8,128]{1,0:T(8,128)S(1)} %copy-done.17, f32[]{:T(128)} %bitcast.8, pred[128,256]{1,0:T(8,128)(4,1)S(1)} %broadcast_and_fusion, ...), kind=kLoop, calls=%fused_computation.210 | loop fusion | flops 11793408 | bytes 12107792 | tf_op jit(solution)/shard_map/reduce_sum | solution.py:105
  99.8 6.9 %collective-permute-start.9 = (f32[1,128,256]{2,1,0:T(8,128)}, f32[1,128,256]{2,1,0:T(8,128)}, u32[]{:S(2)}, u32[]{:S(2)}) collective-permute-start(f32[1,128,256]{2,1,0:T(8,128)} %get-tuple-element.30), channel_id=1, source_target_pairs={{0,4},{4,8},{8,12},{12,16},{16,20},{20,24},{24,28},{28,32},{32,36}... | collective-permute-start | bytes 393224 | tf_op jit(solution)/shard_map/ppermute | solution.py:20
  106.7 313.5 %all-reduce.18.cloned.1.call-done = bf16[4,256,128]{2,1,0:T(8,128)(2,1)} async-done(((bf16[4,256,128]{2,1,0:T(8,128)(2,1)}), bf16[4,256,128]{2,1,0:T(8,128)(2,1)}) %all-reduce.18.cloned.1.call-update) | async-done | bytes 262160 | tf_op jit(solution)/shard_map/psum | solution.py:9
  420.9 9.6 %fusion.105 = f32[8,128]{1,0:T(8,128)S(1)} fusion(f32[8,128,256]{2,1,0:T(8,128)S(1)} %get-tuple-element.17, f32[8,128,256]{2,1,0:T(8,128)} %copy-done.11, f32[]{:T(128)} %bitcast.10, s32[8,128]{1,0:T(8,128)S(1)} %copy-done.17, pred[128,256]{1,0:T(8,128)(4,1)S(1)} %broadcast_and_fusion, pred[8]{0:T(512)(128)(4,1)S(1)} %add_compare_fusion, f32[]{:T(128)} %bitcast.8, ...), kind=kLoop, calls=%fused_computation.145 | loop fusion | flops 10746880 | bytes 11051024 | tf_op jit(solution)/shard_map/reduce_sum | solution.py:105
  430.9 1.4 collective-permute-start.10
  432.3 5.6 %collective-permute-start.11 = (f32[1,128,256]{2,1,0:T(8,128)S(1)}, f32[1,128,256]{2,1,0:T(8,128)S(1)}, u32[]{:S(2)}, u32[]{:S(2)}) collective-permute-start(f32[1,128,256]{2,1,0:T(8,128)S(1)} %get-tuple-element.28), channel_id=1, source_target_pairs={{0,4},{4,8},{8,12},{12,16},{16,20},{20,24},{24,28},{28,32},{32,36}... | collective-permute-start | bytes 393224 | tf_op jit(solution)/shard_map/ppermute | solution.py:20
  438.7 1.5 collective-permute-done.11
  440.2 2.0 fusion.157
  442.2 1.3 collective-permute-start.12
  443.5 6.0 %collective-permute-start.13 = (f32[1,128,256]{2,1,0:T(8,128)S(1)}, f32[1,128,256]{2,1,0:T(8,128)S(1)}, u32[]{:S(2)}, u32[]{:S(2)}) collective-permute-start(f32[1,128,256]{2,1,0:T(8,128)S(1)} %get-tuple-element.26), channel_id=1, source_target_pairs={{0,4},{4,8},{8,12},{12,16},{16,20},{20,24},{24,28},{28,32},{32,36}... | collective-permute-start | bytes 393224 | tf_op jit(solution)/shard_map/ppermute | solution.py:20
  449.9 2.3 collective-permute-done.13
  452.2 3.0 fusion.155
  457.5 6.7 %collective-permute-start.15 = (f32[1,128,256]{2,1,0:T(8,128)S(1)}, f32[1,128,256]{2,1,0:T(8,128)}, u32[]{:S(2)}, u32[]{:S(2)}) collective-permute-start(f32[1,128,256]{2,1,0:T(8,128)S(1)} %get-tuple-element.24), channel_id=1, source_target_pairs={{0,4},{4,8},{8,12},{12,16},{16,20},{20,24},{24,28},{28,32},{32,36}... | collective-permute-start | bytes 393224 | tf_op jit(solution)/shard_map/ppermute | solution.py:20
  464.3 2.1 collective-permute-done.15
  466.4 9.4 %bitcast_multiply_fusion = (f32[8,128,256]{2,1,0:T(8,128)}, f32[8,128,256]{2,1,0:T(8,128)}, f32[8,128,256]{2,1,0:T(8,128)}) fusion(f32[1,8,128,256]{3,2,1,0:T(8,128)} %param.16, bf16[8,128,256]{2,1,0:T(8,128)(2,1)} %all_gather.7, bf16[8,128,256]{2,1,0:T(8,128)(2,1)S(1)} %copy-done.16, f32[8,128,256]{2,1,0:T(8,128)S(1)} %get-tuple-element.17, ...), kind=kLoop, calls=%fused_computation.203 | loop fusion | flops 22806528 | bytes 19935232 | tf_op jit(solution)/shard_map/mul | solution.py:123
  476.6 47.5 %reduce-scatter.3.cloned.1.call-done = f32[8,32,256]{2,1,0:T(8,128)} async-done(((f32[8,128,256]{2,1,0:T(8,128)}), f32[8,32,256]{2,1,0:T(8,128)}) %reduce-scatter.3.cloned.1.call-update) | async-done | bytes 262160 | tf_op jit(solution)/shard_map/reduce_scatter | solution.py:123
  524.0 24.4 %reduce-scatter.5.cloned.1.call-done = f32[8,32,256]{2,1,0:T(8,128)} async-done(((f32[8,128,256]{2,1,0:T(8,128)}), f32[8,32,256]{2,1,0:T(8,128)}) %reduce-scatter.5.cloned.1.call-update) | async-done | bytes 262160 | tf_op jit(solution)/shard_map/reduce_scatter | solution.py:124
  (83 shorter events, 15.6 us)
Async XLA Ops:
  7.2 22.2 %copy-start = (f32[64,4]{0,1:T(4,128)S(1)}, f32[64,4]{0,1:T(4,128)}, u32[]{:S(2)}) copy-start(f32[64,4]{0,1:T(4,128)} %param.20) | copy-start | bytes 3076
  7.2 18.9 %copy-start.22 = (s32[64]{0:T(128)S(1)}, s32[64]{0:T(128)}, u32[]{:S(2)}) copy-start(s32[64]{0:T(128)} %param.21) | copy-start | bytes 772
  7.2 22.3 %copy-start.20 = (bf16[8,32,256]{2,1,0:T(8,128)(2,1)S(1)}, bf16[8,32,256]{2,1,0:T(8,128)(2,1)}, u32[]{:S(2)}) copy-start(bf16[8,32,256]{2,1,0:T(8,128)(2,1)} %param.17) | copy-start | bytes 393220
  7.2 30.7 %copy-start.21 = (bf16[8,32,256]{2,1,0:T(8,128)(2,1)S(1)}, bf16[8,32,256]{2,1,0:T(8,128)(2,1)}, u32[]{:S(2)}) copy-start(bf16[8,32,256]{2,1,0:T(8,128)(2,1)} %param.18) | copy-start | bytes 393220
  7.2 413.0 %all-reduce.18.cloned.1.call-start = ((), (), s32[]{:S(2)}) async-start(), calls=%async_computation.2 | async-start | bytes 524288 | tf_op jit(solution)/shard_map/psum | solution.py:9
  8.3 38.8 %copy-start.1 = (f32[8,128,256]{2,1,0:T(8,128)S(1)}, f32[8,128,256]{2,1,0:T(8,128)}, u32[]{:S(2)}) copy-start(f32[8,128,256]{2,1,0:T(8,128)} %param.15) | copy-start | bytes 3145732
  8.3 38.1 %collective-permute-start.1 = (f32[1,128,256]{2,1,0:T(8,128)S(1)}, f32[1,128,256]{2,1,0:T(8,128)S(1)}, u32[]{:S(2)}, u32[]{:S(2)}) collective-permute-start(f32[1,128,256]{2,1,0:T(8,128)S(1)} %get-tuple-element.37), channel_id=1, source_target_pairs={{4,0},{8,4},{12,8},{16,12},{20,16},{24,20},{28,24},{32,28},{36,32}... | collective-permute-start | bytes 393224 | tf_op jit(solution)/shard_map/ppermute | solution.py:22
  9.8 36.6 %collective-permute-start.3 = (f32[1,128,256]{2,1,0:T(8,128)S(1)}, f32[1,128,256]{2,1,0:T(8,128)S(1)}, u32[]{:S(2)}, u32[]{:S(2)}) collective-permute-start(f32[1,128,256]{2,1,0:T(8,128)S(1)} %get-tuple-element.38), channel_id=1, source_target_pairs={{0,4},{4,8},{8,12},{12,16},{16,20},{20,24},{24,28},{28,32},{32,36}... | collective-permute-start | bytes 393224 | tf_op jit(solution)/shard_map/ppermute | solution.py:20
  17.7 28.7 %collective-permute-start = (f32[1,128,256]{2,1,0:T(8,128)S(1)}, f32[1,128,256]{2,1,0:T(8,128)S(1)}, u32[]{:S(2)}, u32[]{:S(2)}) collective-permute-start(f32[1,128,256]{2,1,0:T(8,128)S(1)} %get-tuple-element.35), channel_id=1, source_target_pairs={{4,0},{8,4},{12,8},{16,12},{20,16},{24,20},{28,24},{32,28},{36,32}... | collective-permute-start | bytes 393224 | tf_op jit(solution)/shard_map/ppermute | solution.py:22
  19.0 27.4 %collective-permute-start.2 = (f32[1,128,256]{2,1,0:T(8,128)S(1)}, f32[1,128,256]{2,1,0:T(8,128)S(1)}, u32[]{:S(2)}, u32[]{:S(2)}) collective-permute-start(f32[1,128,256]{2,1,0:T(8,128)S(1)} %get-tuple-element.36), channel_id=1, source_target_pairs={{0,4},{4,8},{8,12},{12,16},{16,20},{20,24},{24,28},{28,32},{32,36}... | collective-permute-start | bytes 393224 | tf_op jit(solution)/shard_map/ppermute | solution.py:20
  47.1 22.1 %copy-start.8 = (f32[1,8,128,256]{3,2,1,0:T(8,128)S(1)}, f32[1,8,128,256]{3,2,1,0:T(8,128)}, u32[]{:S(2)}) copy-start(f32[1,8,128,256]{3,2,1,0:T(8,128)} %param.13) | copy-start | bytes 3145732
  55.6 17.1 %copy-start.2 = (f32[8,128,256]{2,1,0:T(8,128)}, f32[8,128,256]{2,1,0:T(8,128)S(1)}, u32[]{:S(2)}) copy-start(f32[8,128,256]{2,1,0:T(8,128)S(1)} %get-tuple-element.20) | copy-start | bytes 3145732
  55.6 17.1 %copy-start.4 = (f32[8,128,256]{2,1,0:T(8,128)}, f32[8,128,256]{2,1,0:T(8,128)S(1)}, u32[]{:S(2)}) copy-start(f32[8,128,256]{2,1,0:T(8,128)S(1)} %get-tuple-element.21) | copy-start | bytes 3145732
  55.6 17.1 %copy-start.6 = (f32[8,128,256]{2,1,0:T(8,128)}, f32[8,128,256]{2,1,0:T(8,128)S(1)}, u32[]{:S(2)}) copy-start(f32[8,128,256]{2,1,0:T(8,128)S(1)} %get-tuple-element.22) | copy-start | bytes 3145732
  55.6 17.1 %copy-start.9 = (f32[8,128,256]{2,1,0:T(8,128)}, f32[8,128,256]{2,1,0:T(8,128)S(1)}, u32[]{:S(2)}) copy-start(f32[8,128,256]{2,1,0:T(8,128)S(1)} %get-tuple-element.16) | copy-start | bytes 3145732
  55.6 10.4 %collective-permute-start.4 = (f32[1,128,256]{2,1,0:T(8,128)S(1)}, f32[1,128,256]{2,1,0:T(8,128)S(1)}, u32[]{:S(2)}, u32[]{:S(2)}) collective-permute-start(f32[1,128,256]{2,1,0:T(8,128)S(1)} %get-tuple-element.33), channel_id=1, source_target_pairs={{4,0},{8,4},{12,8},{16,12},{20,16},{24,20},{28,24},{32,28},{36,32}... | collective-permute-start | bytes 393224 | tf_op jit(solution)/shard_map/ppermute | solution.py:22
  56.9 12.3 %collective-permute-start.5 = (f32[1,128,256]{2,1,0:T(8,128)S(1)}, f32[1,128,256]{2,1,0:T(8,128)S(1)}, u32[]{:S(2)}, u32[]{:S(2)}) collective-permute-start(f32[1,128,256]{2,1,0:T(8,128)S(1)} %get-tuple-element.34), channel_id=1, source_target_pairs={{0,4},{4,8},{8,12},{12,16},{16,20},{20,24},{24,28},{28,32},{32,36}... | collective-permute-start | bytes 393224 | tf_op jit(solution)/shard_map/ppermute | solution.py:20
  72.7 14.5 %copy-start.17 = (s32[8,128]{1,0:T(8,128)S(1)}, s32[8,128]{1,0:T(8,128)}, u32[]{:S(2)}) copy-start(s32[8,128]{1,0:T(8,128)} %param.23) | copy-start | bytes 12292
  74.4 9.9 %collective-permute-start.6 = (f32[1,128,256]{2,1,0:T(8,128)}, f32[1,128,256]{2,1,0:T(8,128)}, u32[]{:S(2)}, u32[]{:S(2)}) collective-permute-start(f32[1,128,256]{2,1,0:T(8,128)} %get-tuple-element.31), channel_id=1, source_target_pairs={{4,0},{8,4},{12,8},{16,12},{20,16},{24,20},{28,24},{32,28},{36,32}... | collective-permute-start | bytes 393224 | tf_op jit(solution)/shard_map/ppermute | solution.py:22
  75.7 11.6 %collective-permute-start.7 = (f32[1,128,256]{2,1,0:T(8,128)}, f32[1,128,256]{2,1,0:T(8,128)}, u32[]{:S(2)}, u32[]{:S(2)}) collective-permute-start(f32[1,128,256]{2,1,0:T(8,128)} %get-tuple-element.32), channel_id=1, source_target_pairs={{0,4},{4,8},{8,12},{12,16},{16,20},{20,24},{24,28},{28,32},{32,36}... | collective-permute-start | bytes 393224 | tf_op jit(solution)/shard_map/ppermute | solution.py:20
  84.3 439.8 %reduce-scatter.3.cloned.1.call-start = ((), (), s32[]{:S(2)}) async-start(), calls=%async_computation.3 | async-start | bytes 1310720 | tf_op jit(solution)/shard_map/reduce_scatter | solution.py:123
  98.5 322.4 %collective-permute-start.8 = (f32[1,128,256]{2,1,0:T(8,128)}, f32[1,128,256]{2,1,0:T(8,128)}, u32[]{:S(2)}, u32[]{:S(2)}) collective-permute-start(f32[1,128,256]{2,1,0:T(8,128)} %get-tuple-element.29), channel_id=1, source_target_pairs={{4,0},{8,4},{12,8},{16,12},{20,16},{24,20},{28,24},{32,28},{36,32}... | collective-permute-start | bytes 393224 | tf_op jit(solution)/shard_map/ppermute | solution.py:22
  99.8 321.1 %collective-permute-start.9 = (f32[1,128,256]{2,1,0:T(8,128)}, f32[1,128,256]{2,1,0:T(8,128)}, u32[]{:S(2)}, u32[]{:S(2)}) collective-permute-start(f32[1,128,256]{2,1,0:T(8,128)} %get-tuple-element.30), channel_id=1, source_target_pairs={{0,4},{4,8},{8,12},{12,16},{16,20},{20,24},{24,28},{28,32},{32,36}... | collective-permute-start | bytes 393224 | tf_op jit(solution)/shard_map/ppermute | solution.py:20
  420.9 19.3 %copy-start.7 = (f32[8,128,256]{2,1,0:T(8,128)S(1)}, f32[8,128,256]{2,1,0:T(8,128)}, u32[]{:S(2)}) copy-start(f32[8,128,256]{2,1,0:T(8,128)} %copy-done.6) | copy-start | bytes 3145732
  430.9 7.8 %collective-permute-start.10 = (f32[1,128,256]{2,1,0:T(8,128)S(1)}, f32[1,128,256]{2,1,0:T(8,128)S(1)}, u32[]{:S(2)}, u32[]{:S(2)}) collective-permute-start(f32[1,128,256]{2,1,0:T(8,128)S(1)} %get-tuple-element.27), channel_id=1, source_target_pairs={{4,0},{8,4},{12,8},{16,12},{20,16},{24,20},{28,24},{32,28},{36,32}... | collective-permute-start | bytes 393224 | tf_op jit(solution)/shard_map/ppermute | solution.py:22
  432.3 7.9 %collective-permute-start.11 = (f32[1,128,256]{2,1,0:T(8,128)S(1)}, f32[1,128,256]{2,1,0:T(8,128)S(1)}, u32[]{:S(2)}, u32[]{:S(2)}) collective-permute-start(f32[1,128,256]{2,1,0:T(8,128)S(1)} %get-tuple-element.28), channel_id=1, source_target_pairs={{0,4},{4,8},{8,12},{12,16},{16,20},{20,24},{24,28},{28,32},{32,36}... | collective-permute-start | bytes 393224 | tf_op jit(solution)/shard_map/ppermute | solution.py:20
  442.2 7.8 %collective-permute-start.12 = (f32[1,128,256]{2,1,0:T(8,128)S(1)}, f32[1,128,256]{2,1,0:T(8,128)S(1)}, u32[]{:S(2)}, u32[]{:S(2)}) collective-permute-start(f32[1,128,256]{2,1,0:T(8,128)S(1)} %get-tuple-element.25), channel_id=1, source_target_pairs={{4,0},{8,4},{12,8},{16,12},{20,16},{24,20},{28,24},{32,28},{36,32}... | collective-permute-start | bytes 393224 | tf_op jit(solution)/shard_map/ppermute | solution.py:22
  443.5 8.7 %collective-permute-start.13 = (f32[1,128,256]{2,1,0:T(8,128)S(1)}, f32[1,128,256]{2,1,0:T(8,128)S(1)}, u32[]{:S(2)}, u32[]{:S(2)}) collective-permute-start(f32[1,128,256]{2,1,0:T(8,128)S(1)} %get-tuple-element.26), channel_id=1, source_target_pairs={{0,4},{4,8},{8,12},{12,16},{16,20},{20,24},{24,28},{28,32},{32,36}... | collective-permute-start | bytes 393224 | tf_op jit(solution)/shard_map/ppermute | solution.py:20
  452.2 14.1 %copy-start.16 = (bf16[8,128,256]{2,1,0:T(8,128)(2,1)S(1)}, bf16[8,128,256]{2,1,0:T(8,128)(2,1)}, u32[]{:S(2)}) copy-start(bf16[8,128,256]{2,1,0:T(8,128)(2,1)} %all_gather.6) | copy-start | bytes 1572868
  456.2 8.0 %collective-permute-start.14 = (f32[1,128,256]{2,1,0:T(8,128)S(1)}, f32[1,128,256]{2,1,0:T(8,128)}, u32[]{:S(2)}, u32[]{:S(2)}) collective-permute-start(f32[1,128,256]{2,1,0:T(8,128)S(1)} %get-tuple-element.23), channel_id=1, source_target_pairs={{4,0},{8,4},{12,8},{16,12},{20,16},{24,20},{28,24},{32,28},{36,32}... | collective-permute-start | bytes 393224 | tf_op jit(solution)/shard_map/ppermute | solution.py:22
  457.5 8.8 %collective-permute-start.15 = (f32[1,128,256]{2,1,0:T(8,128)S(1)}, f32[1,128,256]{2,1,0:T(8,128)}, u32[]{:S(2)}, u32[]{:S(2)}) collective-permute-start(f32[1,128,256]{2,1,0:T(8,128)S(1)} %get-tuple-element.24), channel_id=1, source_target_pairs={{0,4},{4,8},{8,12},{12,16},{16,20},{20,24},{24,28},{28,32},{32,36}... | collective-permute-start | bytes 393224 | tf_op jit(solution)/shard_map/ppermute | solution.py:20
  475.8 72.6 %reduce-scatter.5.cloned.1.call-start = ((), (), s32[]{:S(2)}) async-start(), calls=%async_computation.4 | async-start | bytes 1310720 | tf_op jit(solution)/shard_map/reduce_scatter | solution.py:124
  (10 other events, 66.1 us)
Sparse Core Ops, SparseCore 0:
  84.4 335.7 all-reduce.17
  475.9 48.0 reduce-scatter.2
  527.0 21.3 reduce-scatter.4
where the time goes:
time: 556 us; the launch traced here: 555 us
  waiting for transfers between devices  401 us (72%)
  starting transfers between devices  63.4 us (11%)
  other arithmetic  48.2 us (9%)
  between operations  17.5 us (3%)
  blocking collectives  16.2 us (3%)
  local copies, waits for them, and re-layouts  8.46 us (2%)
    psum x1, waiting for transfers between devices, spread(): return lax.psum(jnp.where(mine, shard, jnp.zeros_like(shard)), axis)  314 us
    ppermute x8, starting transfers between devices, with_halo(): lax.ppermute(tail, axis, [(i, (i + 1) % count) for i in range(ends)])  52.7 us
    reduce_scatter x1, waiting for transfers between devices, shards(): lax.psum_scatter(common * latent_own, 'smp', scatter_dimension=1, tiled=T...  47.5 us
    reduce_scatter x1, waiting for transfers between devices, shards(): lax.psum_scatter(common, 'smp', scatter_dimension=1, tiled=True)  24.4 us
    reduce_sum x2, other arithmetic, shards(): residuals.append(jnp.sum(following * onehot, axis=2) - record[turn])  19.1 us
    ppermute x8, waiting for transfers between devices, with_halo(): lax.ppermute(tail, axis, [(i, (i + 1) % count) for i in range(ends)])  12 us
    add x2, other arithmetic, shards(): 2.0 * current - previous + model * applied + wavelet[turn] * point  11.9 us
  transfers between devices with their start and end apart: 19, of which 11 were waited for; matrix products, arithmetic and copies ran while one was open for 3% of the time, Pallas kernels for 0%

commit v1 on v0

v1 whole, which is shorter than its diff:
```python
import functools

import jax
import jax.numpy as jnp
from jax import lax
from jax.experimental import pallas as pl
from jax.experimental.pallas import tpu as pltpu
from jax.sharding import PartitionSpec as P

MESH = pl.DeviceIdType.MESH
F32 = jnp.float32
PAD = 8
T = 8


def kernel(
    sb_h, sn_h, base_h, buoy_h, lat_h, gain_h, bias_h, rec_h, wav, cell, shot, depth,
    img_h, gg_h, bg_h,
    U, W, B, SB, BASE, LAT, PG, RQ, LU, U5, M, Q, CX, CY, CZP, CZM, DB, RB, HIT, AA, IMG, CG, RA, RBUF, RX, RY, RZ, RS, RALL,
    lsem, bar_dummy, hs, hr, ps, pr, gs, gr, rs, rr,
):
    d = lax.axis_index("dom")
    s = lax.axis_index("smp")
    gx, gy, gz = d // 8, (d // 2) % 4, d % 2
    zl, c = s // 2, s % 2
    left, right = ((d + 31) % 32, s), ((d + 1) % 32, s)
    core = (d, 2 * zl + (1 - c))
    zlo = (d, 2 * (1 - zl) + c)
    far = (d, 2 * (1 - zl) + (1 - c))
    xs = [(((gx + k) % 4) * 8 + d % 8, s) for k in (1, 2, 3)]
    ys = [(gx * 8 + ((gy + k) % 4) * 2 + gz, s) for k in (1, 2, 3)]
    zs = (d - gz + (1 - gz), s)

    def load(i, src, dst):
        cp = pltpu.make_async_copy(src, dst, lsem.at[i])
        cp.start()
        return cp

    rows = pl.ds(PAD, 128)
    inner = pl.ds(1, 8)
    ld_u = load(0, sn_h, U.at[0, inner, rows])
    ld_b = load(1, buoy_h, B.at[inner, rows])
    ld_g = load(2, gain_h, PG.at[s, 0])
    ld_c = load(3, bias_h, PG.at[s, 1])
    ld_r = load(4, rec_h.at[:, s], RQ)
    ld_base = load(5, base_h, BASE)
    ld_lat = load(6, lat_h, LAT)
    ld_sb = load(7, sb_h, SB)

    barrier = pltpu.get_barrier_semaphore()
    peers = [left, right, core, zlo, far] + xs + ys
    for p in peers:
        pl.semaphore_signal(barrier, inc=1, device_id=p, device_id_type=MESH)

    zero = jnp.zeros((T, 256), F32)

    def clear(i, _):
        for n in range(4):
            U[n, i, 0:8] = zero
            U[n, i, 136:144] = zero
        for n in range(3):
            W[n, i, 0:8] = zero
            W[n, i, 136:144] = zero
        B[i, 0:8] = zero
        B[i, 136:144] = zero
        return 0

    lax.fori_loop(0, 10, clear, 0)

    picked = shot[0]
    flat = cell[picked]
    cell_x = flat // (128 * 256)
    cell_y = (flat // 256) % 128
    cell_z = flat % 256
    lane = lax.broadcasted_iota(jnp.int32, (T, 256), 1)
    lane_f = lane.astype(F32)
    sub = lax.broadcasted_iota(jnp.int32, (T, 256), 0)
    for j in range(16):
        HIT[T * j : T * j + T] = jnp.where((sub + T * j == cell_y) & (lane == cell_z), 1.0, 0.0)
    dt = jnp.transpose(jnp.concatenate([depth[...].astype(F32), jnp.zeros((120, 128), F32)], axis=0))
    for x in range(8):
        DB[x] = jnp.broadcast_to(dt[:, x : x + 1], (128, 128))

    pl.semaphore_wait(barrier, len(peers))

    def rcopy(src, dst, ss, sr, dev):
        return pltpu.make_async_remote_copy(
            src_ref=src, dst_ref=dst, send_sem=ss, recv_sem=sr, device_id=dev, device_id_type=MESH
        )

    def halo(buf, i):
        a = rcopy(buf.at[8, rows], buf.at[0, rows], hs.at[i, 0], hr.at[i, 0], right)
        b = rcopy(buf.at[1, rows], buf.at[9, rows], hs.at[i, 1], hr.at[i, 1], left)
        a.start()
        b.start()
        return a, b

    def halo_wait(buf, cps):
        for cp in cps:
            cp.wait()

        @pl.when(d == 0)
        def _():
            for j in range(16):
                buf[0, PAD + T * j : PAD + T * j + T] = zero

        @pl.when(d == 31)
        def _():
            for j in range(16):
                buf[9, PAD + T * j : PAD + T * j + T] = zero

    ld_g.wait()
    ld_c.wait()
    p_z = rcopy(PG.at[s], PG.at[s], ps.at[0], pr.at[0], zlo)
    p_c = rcopy(PG.at[s], PG.at[s], ps.at[1], pr.at[1], core)
    p_z.start()
    p_c.start()
    ld_u.wait()
    h_u = halo(U.at[0], 0)
    ld_b.wait()
    h_b = halo(B, 1)

    ld_r.wait()
    mine = (picked // 2 == d).astype(F32)
    odd = (picked % 2).astype(F32)
    for k in range(4):
        r0 = RQ[0, 64 * k : 64 * k + 64].astype(F32)
        r1 = RQ[1, 64 * k : 64 * k + 64].astype(F32)
        RX[k] = (r0 * (1.0 - odd) + r1 * odd) * mine
    r_x = []
    for k in (1, 2, 3):
        cp = rcopy(RX.at[(gx + k) % 4], RX.at[3 + k], rs.at[k - 1], rr.at[k - 1], xs[k - 1])
        cp.start()
        r_x.append(cp)

    ld_base.wait()
    ld_lat.wait()
    ld_sb.wait()

    p_z.wait_recv()
    other = 2 * (1 - zl) + c
    p_f = rcopy(PG.at[other], PG.at[other], ps.at[2], pr.at[2], core)
    p_f.start()
    for cp in h_u:
        cp.wait()
    for cp in h_b:
        cp.wait()

    @pl.when(d == 0)
    def _():
        for j in range(16):
            U[0, 0, PAD + T * j : PAD + T * j + T] = zero
            B[0, PAD + T * j : PAD + T * j + T] = zero

    @pl.when(d == 31)
    def _():
        for j in range(16):
            U[0, 9, PAD + T * j : PAD + T * j + T] = zero
            B[9, PAD + T * j : PAD + T * j + T] = zero

    def coefs(x, _):
        for j in range(17):
            lo = PAD + T * j
            b = B[x + 1, lo : lo + T]
            CY[x, T * j : T * j + T] = 0.5 * (b + B[x + 1, lo - 1 : lo - 1 + T])
            if j < 16:
                CX[x, T * j : T * j + T] = 0.5 * (b + B[x, lo : lo + T])
                zn = jnp.where(lane == 255, 0.0, pltpu.roll(b, 255, 1))
                zp = jnp.where(lane == 0, 0.0, pltpu.roll(b, 1, 1))
                CZP[x, T * j : T * j + T] = 0.5 * (b + zn)
                CZM[x, T * j : T * j + T] = 0.5 * (b + zp)
        return 0

    lax.fori_loop(0, 8, coefs, 0)
    for j in range(16):
        lo = PAD + T * j
        CX[8, T * j : T * j + T] = 0.5 * (B[9, lo : lo + T] + B[8, lo : lo + T])

    r_a = r_x
    for cp in r_a:
        cp.wait()
    for k in range(4):
        sl = pl.ds(16 * k, 16)
        RY[k] = RX[gx, sl] + RX[4, sl] + RX[5, sl] + RX[6, sl]
    r_y = []
    for k in (1, 2, 3):
        cp = rcopy(RY.at[(gy + k) % 4], RY.at[3 + k], rs.at[2 + k], rr.at[2 + k], ys[k - 1])
        cp.start()
        r_y.append(cp)

    p_c.wait()
    p_f.wait()
    p_z.wait_send()

    def model(x, _):
        for j in range(8):
            k, o = j // 2, (j % 2) * 16
            sl = slice(16 * j, 16 * j + 16)
            g = PG[k, 0, x, o : o + 16].astype(F32)
            b = PG[k, 1, x, o : o + 16].astype(F32)
            sq = jnp.tanh(LAT[x, sl] * g + b)
            m = BASE[x, sl] * jnp.exp(0.25 * sq)
            M[x, sl] = m
            Q[x, sl] = m * 0.25 * (1.0 - sq * sq)
        return 0

    lax.fori_loop(0, 8, model, 0)

    def lap(buf, x, j):
        lo = PAD + T * j
        sl = slice(T * j, T * j + T)
        v = buf[x + 1, lo : lo + T]
        t = CX[x + 1, sl] * (buf[x + 2, lo : lo + T] - v) + CX[x, sl] * (buf[x, lo : lo + T] - v)
        t = t + CY[x, T * j + 1 : T * j + 1 + T] * (buf[x + 1, lo + 1 : lo + 1 + T] - v)
        t = t + CY[x, sl] * (buf[x + 1, lo - 1 : lo - 1 + T] - v)
        zn = jnp.where(lane == 255, 0.0, pltpu.roll(v, 255, 1))
        zp = jnp.where(lane == 0, 0.0, pltpu.roll(v, 1, 1))
        return v, t + CZP[x, sl] * (zn - v) + CZM[x, sl] * (zp - v)

    first = d * 8
    for n in range(4):
        if n > 0:
            h = halo(U.at[n], 1 + n)
            halo_wait(U.at[n], h)
        amp = wav[picked, n]

        def step(x, _):
            factor = jnp.where(first + x == cell_x, amp, 0.0)
            for j in range(16):
                sl = slice(T * j, T * j + T)
                lo = PAD + T * j
                v, a = lap(U.at[n], x, j)
                LU[n, x, sl] = a
                prev = SB[x, sl] if n == 0 else U[n - 1, x + 1, lo : lo + T]
                new = 2.0 * v - prev + M[x, sl] * a + factor * HIT[sl]
                if n < 3:
                    U[n + 1, x + 1, lo : lo + T] = new
                else:
                    U5[x, sl] = new
            return 0

        lax.fori_loop(0, 8, step, 0)
        if n == 0:
            for cp in r_y:
                cp.wait()
            for k in range(2):
                sl = pl.ds(8 * k, 8)
                RZ[k] = RY[gy, sl] + RY[4, sl] + RY[5, sl] + RY[6, sl]
            r_z = rcopy(RZ.at[1 - gz], RZ.at[2], rs.at[6], rr.at[6], zs)
            r_z.start()
        if n == 1:
            r_z.wait()
            RALL[s] = RZ[gz] + RZ[2]
            r_s = []
            for i, p in enumerate((core, zlo, far)):
                cp = rcopy(RALL.at[s], RALL.at[s], rs.at[7 + i], rr.at[7 + i], p)
                cp.start()
                r_s.append(cp)
        if n == 2:
            for cp in r_s:
                cp.wait()
            rt = jnp.transpose(jnp.concatenate([RALL[k] for k in range(4)] + [jnp.zeros((96, 128), F32)], axis=0))
            for k in range(4):
                for x in range(8):
                    RB[k, x] = jnp.broadcast_to(rt[:, 8 * k + x : 8 * k + x + 1], (128, 128))

    for i, n in enumerate((3, 2, 1, 0)):
        if i > 0:
            h = halo(W.at[i - 1], 4 + i)
            halo_wait(W.at[i - 1], h)

        def back(x, _):
            for j in range(16):
                sl = slice(T * j, T * j + T)
                lo = PAD + T * j
                dd = DB[x, sl]
                rr_ = RB[n, x, sl]
                dd = jnp.concatenate([dd, dd], axis=1)
                rr_ = jnp.concatenate([rr_, rr_], axis=1)
                u = U5[x, sl] if n == 3 else U[n + 1, x + 1, lo : lo + T]
                a = jnp.where(lane_f == dd, u - rr_, 0.0)
                if i > 0:
                    _, t = lap(W.at[i - 1], x, j)
                    a = a + t + 2.0 * AA[(i - 1) % 3, x, sl]
                if i > 1:
                    a = a - AA[(i - 2) % 3, x, sl]
                img = a * LU[n, x, sl]
                if i > 0:
                    img = img + IMG[x, sl]
                IMG[x, sl] = img
                if i < 3:
                    AA[i % 3, x, sl] = a
                    W[i, x + 1, lo : lo + T] = M[x, sl] * a
                else:
                    com = img * Q[x, sl]
                    k, o = j // 4, (j % 4) * 8
                    CG[k, 1, x, o : o + 8] = com
                    CG[k, 0, x, o : o + 8] = com * LAT[x, sl]
            return 0

        lax.fori_loop(0, 8, back, 0)

    out_i = load(0, IMG, img_h)

    g_c = []
    for i in range(2):
        cp = rcopy(CG.at[2 * i + (1 - c)], RA.at[i], gs.at[i], gr.at[i], core)
        cp.start()
        g_c.append(cp)

    def add(dst, src):
        def body(x, _):
            for f in range(2):
                dst[f, x] = dst[f, x] + src[f, x]
            return 0

        lax.fori_loop(0, 8, body, 0)

    for cp in g_c:
        cp.wait()
    add(CG.at[2 * (1 - zl) + c], RA.at[1 - zl])
    g_z = rcopy(CG.at[2 * (1 - zl) + c], RBUF, gs.at[2], gr.at[2], zlo)
    g_z.start()
    add(CG.at[s], RA.at[zl])
    g_z.wait()
    add(CG.at[s], RBUF)
    out_g = load(1, CG.at[s, 0], gg_h)
    out_b = load(2, CG.at[s, 1], bg_h)
    out_i.wait()
    out_g.wait()
    out_b.wait()


def shards(
    state_before, state_now, base_model, buoyancy, latent, flow_gain, flow_bias, records, source_wavelet, source_cell,
    shot, receiver_depth,
):
    any_ = pl.BlockSpec(memory_space=pl.ANY)
    smem = pl.BlockSpec(memory_space=pltpu.SMEM)
    vmem = pl.BlockSpec(memory_space=pltpu.VMEM)
    field = (8, 128, 256)
    halo = (10, 144, 256)
    img, gg, bg = pl.pallas_call(
        kernel,
        out_shape=(
            jax.ShapeDtypeStruct(field, F32),
            jax.ShapeDtypeStruct((8, 32, 256), F32),
            jax.ShapeDtypeStruct((8, 32, 256), F32),
        ),
        in_specs=[any_] * 8 + [smem] * 3 + [vmem],
        out_specs=(any_, any_, any_),
        scratch_shapes=[
            pltpu.VMEM((4,) + halo, F32),
            pltpu.VMEM((3,) + halo, F32),
            pltpu.VMEM(halo, F32),
            pltpu.VMEM(field, F32),
            pltpu.VMEM(field, F32),
            pltpu.VMEM(field, F32),
            pltpu.VMEM((4, 2, 8, 32, 256), jnp.bfloat16),
            pltpu.VMEM((2, 256, 128), jnp.bfloat16),
            pltpu.VMEM((4,) + field, F32),
            pltpu.VMEM(field, F32),
            pltpu.VMEM(field, F32),
            pltpu.VMEM(field, F32),
            pltpu.VMEM((9, 128, 256), F32),
            pltpu.VMEM((8, 136, 256), F32),
            pltpu.VMEM(field, F32),
            pltpu.VMEM(field, F32),
            pltpu.VMEM((8, 128, 128), F32),
            pltpu.VMEM((4, 8, 128, 128), F32),
            pltpu.VMEM((128, 256), F32),
            pltpu.VMEM((3,) + field, F32),
            pltpu.VMEM(field, F32),
            pltpu.VMEM((4, 2, 8, 32, 256), F32),
            pltpu.VMEM((2, 2, 8, 32, 256), F32),
            pltpu.VMEM((2, 8, 32, 256), F32),
            pltpu.VMEM((7, 64, 128), F32),
            pltpu.VMEM((7, 16, 128), F32),
            pltpu.VMEM((3, 8, 128), F32),
            pltpu.VMEM((1, 8, 128), F32),
            pltpu.VMEM((4, 8, 128), F32),
            pltpu.SemaphoreType.DMA((8,)),
            pltpu.SemaphoreType.REGULAR,
            pltpu.SemaphoreType.DMA((8, 2)),
            pltpu.SemaphoreType.DMA((8, 2)),
            pltpu.SemaphoreType.DMA((3,)),
            pltpu.SemaphoreType.DMA((3,)),
            pltpu.SemaphoreType.DMA((3,)),
            pltpu.SemaphoreType.DMA((3,)),
            pltpu.SemaphoreType.DMA((10,)),
            pltpu.SemaphoreType.DMA((10,)),
        ],
        compiler_params=pltpu.CompilerParams(
            collective_id=1, has_side_effects=True, vmem_limit_bytes=58 << 20
        ),
        name="flow_gradient",
    )(
        state_before[0], state_now[0], base_model, buoyancy, latent[0], flow_gain, flow_bias, records, source_wavelet,
        source_cell, shot, receiver_depth,
    )
    return img[None], gg, bg


def solution(mesh):
    in_specs = (
        P("smp", "dom", None, None),
        P("smp", "dom", None, None),
        P("dom", None, None),
        P("dom", None, None),
        P("smp", "dom", None, None),
        P("dom", "smp", None),
        P("dom", "smp", None),
        P("dom", None, None, None),
        P(),
        P(),
        P(),
        P("dom", None),
    )
    out_specs = (P("smp", "dom", None, None), P("dom", "smp", None), P("dom", "smp", None))
    return jax.shard_map(shards, mesh=mesh, in_specs=in_specs, out_specs=out_specs, check_vma=False)
```

time: 556 us -> 111 us (0.20)
  waiting for transfers between devices: 401 us -> 0 us
  Pallas kernels: 0 us -> 104 us
  starting transfers between devices: 63.4 us -> 0 us
  other arithmetic: 48.2 us -> 0 us
  blocking collectives: 16.2 us -> 0 us
  between operations: 17.5 us -> 1.3 us
    psum x1 -> x0, waiting for transfers between devices: 314 us -> none  [spread(): return lax.psum(jnp.where(mine, shard, jnp.zeros_like(shard)), axis)]
    pallas_call x0 -> x1, Pallas kernels: none -> 104 us  [shards(): pl.pallas_call(kernel, out_shape=(jax.ShapeDtypeStruct(field, F32), jax.S...]
    reduce_scatter x2 -> x0, waiting for transfers between devices: 71.8 us -> none  [the longest x1 47.5 us: shards(): lax.psum_scatter(common * latent_own, 'smp', scatter_dimension=1, tiled=T...]
    ppermute x16 -> x0, starting transfers between devices: 63.3 us -> none  [the longest x8 52.7 us: with_halo(): lax.ppermute(tail, axis, [(i, (i + 1) % count) for i in range(ends)])]
    reduce_sum x2 -> x0, other arithmetic: 19.1 us -> none  [shards(): residuals.append(jnp.sum(following * onehot, axis=2) - record[turn])]
    all_gather x2 -> x0, blocking collectives: 16.2 us -> none  [the longest x1 8.5 us: shards(): lax.all_gather(flow_gain, 'smp', axis=1, tiled=True)]
    ppermute x16 -> x0, waiting for transfers between devices: 15.1 us -> none  [the longest x8 12 us: with_halo(): lax.ppermute(tail, axis, [(i, (i + 1) % count) for i in range(ends)])]
    mul x4 -> x0, other arithmetic: 14.7 us -> none  [the longest x1 9.41 us: shards(): common * latent_own]
  transfers between devices with their start and end apart: 19 -> 0, of which waited for: 11 -> 0; matrix products, arithmetic and copies ran while one was open for 3% -> 0% of each run, Pallas kernels for 0% -> 0%
where the time goes in v1:
time: 111 us
  Pallas kernels  104 us (94%)
  local copies, waits for them, and re-layouts  5.44 us (5%)
  between operations  1.3 us (1%)
    pallas_call x1, Pallas kernels, shards(): pl.pallas_call(kernel, out_shape=(jax.ShapeDtypeStruct(field, F32), jax.S...  104 us
    unnamed x10, local copies, waits for them, and re-layouts  5.44 us

profile of v1, /device:TPU:1, one launch (start us, length us, event | category | flops | bytes accessed | tf_op | source)
XLA Modules:
  0.0 110.9 jit_solution(12679194461578119051)
XLA Ops:
  1.3 0.0 copy-start.2
  1.3 0.7 copy-done.2
  2.0 0.7 copy.15.wav
  2.7 104.1 %flow_gradient.1 = (f32[8,128,256]{2,1,0:T(8,128)}, f32[8,32,256]{2,1,0:T(8,128)}, f32[8,32,256]{2,1,0:T(8,128)}) custom-call(f32[8,128,256]{2,1,0:T(8,128)} %bitcast.5, f32[8,128,256]{2,1,0:T(8,128)} %bitcast.6, f32[8,128,256]{2,1,0:T(8,128)} %base_h.1, f32[8,128,256]{2,1,0:T(8,128)} %buoy_h.1, f32[8,128,256]{2,1,0:T(8,128)} %bitcast.7, ...), custom_call_target="tpu_custom_call" | custom-call | tf_op jit(solution)/shard_map/flow_gradient/pallas_call | solution.py:343
  106.8 0.0 copy-start.1
  106.8 2.3 %copy.20 = f32[1,8,128,256]{3,2,1,0:T(8,128)} copy(f32[1,8,128,256]{3,2,1,0:T(8,128)} %bitcast.4) | data formatting | bytes 2097152
  109.1 0.0 copy-done.1
  109.1 0.0 copy-start
  109.1 0.7 copy.21
  109.8 0.3 copy-done
  110.2 0.7 copy.22
Async XLA Ops:
  1.3 0.7 copy-start.2
  106.8 2.3 %copy-start.1 = (f32[8,32,256]{2,1,0:T(8,128)S(1)}, f32[8,32,256]{2,1,0:T(8,128)}, u32[]{:S(2)}) copy-start(f32[8,32,256]{2,1,0:T(8,128)} %get-tuple-element.13) | copy-start | bytes 786436
  109.1 1.0 copy-start

commit v2 on v1

--- a/solution.py
+++ b/solution.py
@@ -2,22 +2,44 @@
 
 import jax
 import jax.numpy as jnp
+import numpy as np
 from jax import lax
 from jax.experimental import pallas as pl
 from jax.experimental.pallas import tpu as pltpu
 from jax.sharding import PartitionSpec as P
 
 MESH = pl.DeviceIdType.MESH
+I32 = jnp.int32
+
+
+def ball(radius):
+    return [(a, b) for a in range(-radius, radius + 1) for b in range(abs(a) - radius, radius - abs(a) + 1)]
+
+
+def near(plane):
+    return [(plane + a, y, z) for a in range(-3, 4) for y, z in ball(3 - abs(a))]
+
+
+def tables():
+    lists = [near(x) for x in range(8)]
+    pick = np.zeros((128, 64 * len(lists)), np.float32)
+    shift = np.zeros((8, 64 * len(lists)), np.float32)
+    for i, cells in enumerate(lists):
+        cells = cells + [cells[0]] * (64 - len(cells))
+        for j, (p, y, z) in enumerate(cells):
+            pick[16 * (y + 3) + p + 3, 64 * i + j] = 1.0
+            shift[:, 64 * i + j] = z
+    return pick, shift
 F32 = jnp.float32
 PAD = 8
 T = 8
 
 
 def kernel(
-    sb_h, sn_h, base_h, buoy_h, lat_h, gain_h, bias_h, rec_h, wav, cell, shot, depth,
+    sb_h, sn_h, base_h, buoy_h, lat_h, gain_h, bias_h, rec_h, wav, cell, shot, depth, pick, shift,
     img_h, gg_h, bg_h,
-    U, W, B, SB, BASE, LAT, PG, RQ, LU, U5, M, Q, CX, CY, CZP, CZM, DB, RB, HIT, AA, IMG, CG, RA, RBUF, RX, RY, RZ, RS, RALL,
-    lsem, bar_dummy, hs, hr, ps, pr, gs, gr, rs, rr,
+    U, W, B, SB, BASE, LAT, PG, RQ, LU, U5, M, Q, CX, CY, CZP, CZM, DB, RB, HIT, AA, IMG, CA, CB, GA, GB, CG, RA, RBUF, RX, RY, RZ, RS, RALL, DS, DH, IDX, INV,
+    lsem, bar_dummy, hs, hr, ps, pr, gs, gr, rs, rr, ds_, dr_,
 ):
     d = lax.axis_index("dom")
     s = lax.axis_index("smp")
@@ -109,6 +131,11 @@
             for j in range(16):
                 buf[9, PAD + T * j : PAD + T * j + T] = zero
 
+    DS[...] = depth[...].astype(F32)
+    d_l = rcopy(DS, DH.at[1], ds_.at[0], dr_.at[0], left)
+    d_r = rcopy(DS, DH.at[0], ds_.at[1], dr_.at[1], right)
+    d_l.start()
+    d_r.start()
     ld_g.wait()
     ld_c.wait()
     p_z = rcopy(PG.at[s], PG.at[s], ps.at[0], pr.at[0], zlo)
@@ -187,6 +214,30 @@
         cp = rcopy(RY.at[(gy + k) % 4], RY.at[3 + k], rs.at[2 + k], rr.at[2 + k], ys[k - 1])
         cp.start()
         r_y.append(cp)
+
+    d_l.wait()
+    d_r.wait()
+    near_d = jnp.concatenate([DH[0, 5:8], DS[...], DH[1, 0:3], jnp.zeros((2, 128), F32)], axis=0)
+    rolled = [near_d if y == 0 else pltpu.roll(near_d, (-y) % 128, 1) for y in range(-3, 4)]
+    key = jnp.transpose(jnp.concatenate(rolled + [jnp.zeros((16, 128), F32)], axis=0)).astype(jnp.bfloat16)
+    idx = jnp.dot(key, pick[...], preferred_element_type=F32) + shift[0:1, :]
+    idx = jnp.clip(idx, 0.0, 255.0).astype(I32)
+    for q in range(4):
+        IDX[q] = idx[:, 128 * q : 128 * q + 128]
+
+    def invert(t, _):
+        at = pl.ds(pl.multiple_of(32 * s + T * t, T), T)
+        for q in range(4):
+            tile = IDX[q, at]
+            for h in range(2):
+                inv = jnp.full((T, 256), -1, I32)
+                for j in range(63):
+                    jj = 64 * h + j
+                    inv = jnp.where(lane == tile[:, jj : jj + 1], jj, inv)
+                INV[2 * q + h, t] = inv
+        return 0
+
+    lax.fori_loop(0, 4, invert, 0)
 
     p_c.wait()
     p_f.wait()
@@ -293,39 +344,69 @@
                     W[i, x + 1, lo : lo + T] = M[x, sl] * a
                 else:
                     com = img * Q[x, sl]
-                    k, o = j // 4, (j % 4) * 8
-                    CG[k, 1, x, o : o + 8] = com
-                    CG[k, 0, x, o : o + 8] = com * LAT[x, sl]
+                    CB[x, sl] = com
+                    CA[x, sl] = com * LAT[x, sl]
             return 0
 
         lax.fori_loop(0, 8, back, 0)
 
     out_i = load(0, IMG, img_h)
 
+    lane1 = lax.broadcasted_iota(I32, (T, 128), 1)
+
+    def compact(k):
+        def body(t, _):
+            at = pl.ds(pl.multiple_of(32 * k + T * t, T), T)
+            for q in range(4):
+                tile = IDX[q, at]
+                low, tile = tile < 128, tile & 127
+                for f, src in enumerate((CA, CB)):
+                    halves = []
+                    for x in (2 * q, 2 * q + 1):
+                        v = src[x, at]
+                        g0 = jnp.take_along_axis(v[:, :128], tile, axis=1, mode="promise_in_bounds")
+                        g1 = jnp.take_along_axis(v[:, 128:], tile, axis=1, mode="promise_in_bounds")
+                        halves.append(jnp.where(low, g0, g1))
+                    CG[k, f, q, t] = jnp.where(lane1 < 64, halves[0], halves[1])
+            return 0
+
+        lax.fori_loop(0, 4, body, 0)
+
     g_c = []
-    for i in range(2):
+    for i in (1 - zl, zl):
+        compact(2 * i + (1 - c))
         cp = rcopy(CG.at[2 * i + (1 - c)], RA.at[i], gs.at[i], gr.at[i], core)
         cp.start()
         g_c.append(cp)
-
-    def add(dst, src):
-        def body(x, _):
-            for f in range(2):
-                dst[f, x] = dst[f, x] + src[f, x]
-            return 0
-
-        lax.fori_loop(0, 8, body, 0)
-
-    for cp in g_c:
-        cp.wait()
-    add(CG.at[2 * (1 - zl) + c], RA.at[1 - zl])
-    g_z = rcopy(CG.at[2 * (1 - zl) + c], RBUF, gs.at[2], gr.at[2], zlo)
+    pair = 2 * (1 - zl) + c
+    compact(pair)
+    g_c[0].wait()
+    for f in range(2):
+        for q in range(4):
+            CG[pair, f, q] = CG[pair, f, q] + RA[1 - zl, f, q]
+    g_z = rcopy(CG.at[pair], RBUF, gs.at[2], gr.at[2], zlo)
     g_z.start()
-    add(CG.at[s], RA.at[zl])
+    g_c[1].wait()
     g_z.wait()
-    add(CG.at[s], RBUF)
-    out_g = load(1, CG.at[s, 0], gg_h)
-    out_b = load(2, CG.at[s, 1], bg_h)
+
+    def spread(t, _):
+        at = pl.ds(pl.multiple_of(32 * s + T * t, T), T)
+        to = pl.ds(pl.multiple_of(T * t, T), T)
+        for q in range(4):
+            for f, src, out in ((0, CA, GA), (1, CB, GB)):
+                v = RA[zl, f, q, t] + RBUF[f, q, t]
+                for x in (2 * q, 2 * q + 1):
+                    inv = INV[x, t]
+                    have, inv = inv >= 0, inv & 127
+                    g0 = jnp.take_along_axis(v, inv[:, :128], axis=1, mode="promise_in_bounds")
+                    g1 = jnp.take_along_axis(v, inv[:, 128:], axis=1, mode="promise_in_bounds")
+                    g = jnp.concatenate([g0, g1], axis=1)
+                    out[x, to] = src[x, at] + jnp.where(have, g, 0.0)
+        return 0
+
+    lax.fori_loop(0, 4, spread, 0)
+    out_g = load(1, GA, gg_h)
+    out_b = load(2, GB, bg_h)
     out_i.wait()
     out_g.wait()
     out_b.wait()
@@ -340,6 +421,7 @@
     vmem = pl.BlockSpec(memory_space=pltpu.VMEM)
     field = (8, 128, 256)
     halo = (10, 144, 256)
+    pick, shift = tables()
     img, gg, bg = pl.pallas_call(
         kernel,
         out_shape=(
@@ -347,7 +429,7 @@
             jax.ShapeDtypeStruct((8, 32, 256), F32),
             jax.ShapeDtypeStruct((8, 32, 256), F32),
         ),
-        in_specs=[any_] * 8 + [smem] * 3 + [vmem],
+        in_specs=[any_] * 8 + [smem] * 3 + [vmem] * 3,
         out_specs=(any_, any_, any_),
         scratch_shapes=[
             pltpu.VMEM((4,) + halo, F32),
@@ -371,14 +453,22 @@
             pltpu.VMEM((128, 256), F32),
             pltpu.VMEM((3,) + field, F32),
             pltpu.VMEM(field, F32),
-            pltpu.VMEM((4, 2, 8, 32, 256), F32),
-            pltpu.VMEM((2, 2, 8, 32, 256), F32),
-            pltpu.VMEM((2, 8, 32, 256), F32),
+            pltpu.VMEM(field, F32),
+            pltpu.VMEM(field, F32),
+            pltpu.VMEM((8, 32, 256), F32),
+            pltpu.VMEM((8, 32, 256), F32),
+            pltpu.VMEM((4, 2, 4, 4, 8, 128), F32),
+            pltpu.VMEM((2, 2, 4, 4, 8, 128), F32),
+            pltpu.VMEM((2, 4, 4, 8, 128), F32),
             pltpu.VMEM((7, 64, 128), F32),
             pltpu.VMEM((7, 16, 128), F32),
             pltpu.VMEM((3, 8, 128), F32),
             pltpu.VMEM((1, 8, 128), F32),
             pltpu.VMEM((4, 8, 128), F32),
+            pltpu.VMEM((8, 128), F32),
+            pltpu.VMEM((2, 8, 128), F32),
+            pltpu.VMEM((4, 128, 128), I32),
+            pltpu.VMEM((8, 4, 8, 256), I32),
             pltpu.SemaphoreType.DMA((8,)),
             pltpu.SemaphoreType.REGULAR,
             pltpu.SemaphoreType.DMA((8, 2)),
@@ -389,6 +479,8 @@
             pltpu.SemaphoreType.DMA((3,)),
             pltpu.SemaphoreType.DMA((10,)),
             pltpu.SemaphoreType.DMA((10,)),
+            pltpu.SemaphoreType.DMA((2,)),
+            pltpu.SemaphoreType.DMA((2,)),
         ],
         compiler_params=pltpu.CompilerParams(
             collective_id=1, has_side_effects=True, vmem_limit_bytes=58 << 20
@@ -396,7 +488,7 @@
         name="flow_gradient",
     )(
         state_before[0], state_now[0], base_model, buoyancy, latent[0], flow_gain, flow_bias, records, source_wavelet,
-        source_cell, shot, receiver_depth,
+        source_cell, shot, receiver_depth, jnp.asarray(pick, jnp.bfloat16), jnp.asarray(shift),
     )
     return img[None], gg, bg
 

time: 111 us -> 107 us (0.964); the launches traced: 111 us -> 106 us
  Pallas kernels: 104 us -> 98.8 us
    pallas_call x1, Pallas kernels: 104 us -> 98.8 us  [shards(): pl.pallas_call(kernel, out_shape=(jax.ShapeDtypeStruct(field, F32), jax.S...]
where the time goes in v2:
time: 107 us; the launch traced here: 106 us
  Pallas kernels  98.8 us (92%)
  local copies, waits for them, and re-layouts  5.44 us (5%)
  between operations  1.3 us (1%)
    pallas_call x1, Pallas kernels, shards(): pl.pallas_call(kernel, out_shape=(jax.ShapeDtypeStruct(field, F32), jax.S...  98.8 us
    unnamed x10, local copies, waits for them, and re-layouts  5.44 us

profile of v2, /device:TPU:1, one launch (start us, length us, event | category | flops | bytes accessed | tf_op | source)
XLA Modules:
  0.0 105.5 jit_solution(6432528811310950228)
XLA Ops:
  1.3 0.0 copy-start.2
  1.3 0.7 copy-done.2
  2.0 0.7 copy.17.wav
  2.7 98.8 %flow_gradient.1 = (f32[8,128,256]{2,1,0:T(8,128)}, f32[8,32,256]{2,1,0:T(8,128)}, f32[8,32,256]{2,1,0:T(8,128)}) custom-call(f32[8,128,256]{2,1,0:T(8,128)} %bitcast.5, f32[8,128,256]{2,1,0:T(8,128)} %bitcast.6, f32[8,128,256]{2,1,0:T(8,128)} %base_h.1, f32[8,128,256]{2,1,0:T(8,128)} %buoy_h.1, f32[8,128,256]{2,1,0:T(8,128)} %bitcast.7, ...), custom_call_target="tpu_custom_call" | custom-call | tf_op jit(solution)/shard_map/flow_gradient/pallas_call | solution.py:425
  101.4 0.0 copy-start.1
  101.5 2.3 %copy.22 = f32[1,8,128,256]{3,2,1,0:T(8,128)} copy(f32[1,8,128,256]{3,2,1,0:T(8,128)} %bitcast.4) | data formatting | bytes 2097152
  103.8 0.0 copy-done.1
  103.8 0.0 copy-start
  103.8 0.7 copy.23
  104.5 0.3 copy-done
  104.8 0.7 copy.24
Async XLA Ops:
  1.3 0.7 copy-start.2
  101.4 2.3 %copy-start.1 = (f32[8,32,256]{2,1,0:T(8,128)S(1)}, f32[8,32,256]{2,1,0:T(8,128)}, u32[]{:S(2)}) copy-start(f32[8,32,256]{2,1,0:T(8,128)} %get-tuple-element.13) | copy-start | bytes 786436
  103.8 1.0 copy-start

commit v3 on v2

v3 whole, which is shorter than its diff:
```python
import functools

import jax
import jax.numpy as jnp
import numpy as np
from jax import lax
from jax.experimental import pallas as pl
from jax.experimental.pallas import tpu as pltpu
from jax.sharding import PartitionSpec as P

MESH = pl.DeviceIdType.MESH
I32 = jnp.int32


def ball(radius):
    return [(a, b) for a in range(-radius, radius + 1) for b in range(abs(a) - radius, radius - abs(a) + 1)]


def near(plane):
    return [(plane + a, y, z) for a in range(-3, 4) for y, z in ball(3 - abs(a))]


def across(height):
    radius = {1: {0: 2, -1: 2, 1: 1, -2: 1, 2: 0, -3: 0}, 2: {0: 1, -1: 1, -2: 1, 1: 0, -3: 0}, 3: {0: 0, -2: 0, -3: 0}}
    return [(p, y, z) for p, r in radius[height].items() for y, z in ball(r)]


COUNTS = [len(across(h)) for h in (1, 2, 3)]
STARTS = [sum(COUNTS[:h]) for h in range(4)]


SPARE = 58
USCALE = 32767.0 / 6.0
BSCALE = 65532.0


def tables():
    up = sum((across(h) for h in (1, 2, 3)), [])
    down = [(-1 - p, y, z) for p, y, z in up]
    right = [[(p + 8, y, z) for p, y, z in cells] for cells in (up, down)]
    lists = [near(x) for x in range(8)] + [down, right[0], up, right[1]]
    pick = np.zeros((128, 64 * len(lists)), np.float32)
    shift = np.zeros((8, 64 * len(lists)), np.float32)
    for i, cells in enumerate(lists):
        if i >= 8:
            cells = cells + [{8: (-1, 0, 0), 9: (8, 0, 0), 10: (0, 0, 0), 11: (7, 0, 0)}[i]]
        cells = cells + [cells[0]] * (64 - len(cells))
        for j, (p, y, z) in enumerate(cells):
            pick[16 * (y + 3) + p + 3, 64 * i + j] = 1.0
            shift[:, 64 * i + j] = z
    return pick, shift


F32 = jnp.float32
PAD = 8
T = 8


def kernel(
    sb_h, sn_h, base_h, buoy_h, lat_h, gain_h, bias_h, rec_h, wav, cell, shot, depth, pick, shift,
    img_h, gg_h, bg_h,
    U, B, SB, BASE, LAT, PG, RQ, LU, AA, M, Q, CX, CY, CZP, CZM, DB, RB, HIT, IMG, CA, CB, GA, GB, CG, RA, RBUF,
    RX, RY, RZ, RALL, DS, DH, IDX, INV, SIDX, RIDX, INVH, SE, RE, SG, RG, KT, SR, RR,
    lsem, es, er, hs, hr, ps, pr, gs, gr, rs, rr, ds_, dr_,
):
    d = lax.axis_index("dom")
    s = lax.axis_index("smp")
    gx, gy, gz = d // 8, (d // 2) % 4, d % 2
    zl, c = s // 2, s % 2
    left, right = ((d + 31) % 32, s), ((d + 1) % 32, s)
    core = (d, 2 * zl + (1 - c))
    zlo = (d, 2 * (1 - zl) + c)
    far = (d, 2 * (1 - zl) + (1 - c))
    xs = [(((gx + k) % 4) * 8 + d % 8, s) for k in (1, 2, 3)]
    ys = [(gx * 8 + ((gy + k) % 4) * 2 + gz, s) for k in (1, 2, 3)]
    zs = (d - gz + (1 - gz), s)

    def load(i, src, dst):
        cp = pltpu.make_async_copy(src, dst, lsem.at[i])
        cp.start()
        return cp

    rows = pl.ds(PAD, 128)
    own = pl.ds(3, 8)
    ld_g = load(2, gain_h, PG.at[s, 0])
    ld_c = load(3, bias_h, PG.at[s, 1])
    ld_u = load(0, sn_h, U.at[0, own, rows])
    ld_b = load(1, buoy_h, B.at[own, rows])
    ld_r = load(4, rec_h.at[:, s], RQ)
    ld_base = load(5, base_h, BASE)
    ld_lat = load(6, lat_h, LAT)
    ld_sb = load(7, sb_h, SB)

    barrier = pltpu.get_barrier_semaphore()
    peers = [left, right, core, zlo, far] + xs + ys
    for p in peers:
        pl.semaphore_signal(barrier, inc=1, device_id=p, device_id_type=MESH)

    def rcopy(src, dst, ss, sr, dev):
        return pltpu.make_async_remote_copy(
            src_ref=src, dst_ref=dst, send_sem=ss, recv_sem=sr, device_id=dev, device_id_type=MESH
        )

    def loop(n, body):
        def run(i, _):
            body(i)
            return 0

        lax.fori_loop(0, n, run, 0)

    zero = jnp.zeros((T, 256), F32)
    lane = lax.broadcasted_iota(I32, (T, 256), 1)
    lane1 = lax.broadcasted_iota(I32, (T, 128), 1)
    lane_f = lane.astype(F32)

    def tile(j):
        return slice(T * j, T * j + T)

    def padded(j):
        return slice(PAD + T * j, PAD + T * j + T)

    def twice(v):
        return jnp.concatenate([v, v], axis=1)

    def clear(i):
        for n in range(4):
            U[n, i, 0:8] = zero
            U[n, i, 136:144] = zero
        B[i, 0:8] = zero
        B[i, 136:144] = zero
        for j in range(16):
            AA[4, i, tile(j)] = zero

    loop(14, clear)

    picked = shot[0]
    flat = cell[picked]
    cell_x = flat // (128 * 256)
    cell_y = (flat // 256) % 128
    cell_z = flat % 256
    sub = lax.broadcasted_iota(I32, (T, 256), 0)
    for j in range(16):
        HIT[tile(j)] = jnp.where((sub + T * j == cell_y) & (lane == cell_z), 1.0, 0.0)
    DS[...] = depth[...].astype(F32)

    ld_u.wait()
    ld_b.wait()
    for e, p in enumerate((0, 7)):
        for j in range(8):
            sl = slice(16 * j, 16 * j + 16)
            at = slice(PAD + 16 * j, PAD + 16 * j + 16)
            SE[e, 0, sl] = jnp.round(U[0, p + 3, at] * USCALE).astype(I32).astype(jnp.int16)
            SE[e, 1, sl] = jnp.round((B[p + 3, at] - 1.0) * BSCALE).astype(I32).astype(jnp.int16)

    ld_g.wait()
    ld_c.wait()
    pl.semaphore_wait(barrier, len(peers))

    d_l = rcopy(DS, DH.at[1], ds_.at[0], dr_.at[0], left)
    d_r = rcopy(DS, DH.at[0], ds_.at[1], dr_.at[1], right)
    d_l.start()
    d_r.start()
    p_z = rcopy(PG.at[s], PG.at[s], ps.at[0], pr.at[0], zlo)
    p_c = rcopy(PG.at[s], PG.at[s], ps.at[1], pr.at[1], core)
    e_l = rcopy(SE.at[0], RE.at[1], es.at[0], er.at[0], left)
    e_r = rcopy(SE.at[1], RE.at[0], es.at[1], er.at[1], right)
    e_l.start()
    e_r.start()
    p_z.start()
    p_c.start()

    ld_r.wait()
    mine = (picked // 2 == d).astype(F32)
    odd = (picked % 2).astype(F32)
    for k in range(4):
        r0 = RQ[0, 64 * k : 64 * k + 64].astype(F32)
        r1 = RQ[1, 64 * k : 64 * k + 64].astype(F32)
        RX[k] = (r0 * (1.0 - odd) + r1 * odd) * mine
    r_x = []
    for k in (1, 2, 3):
        cp = rcopy(RX.at[(gx + k) % 4], RX.at[3 + k], rs.at[k - 1], rr.at[k - 1], xs[k - 1])
        cp.start()
        r_x.append(cp)

    def coef_yz(p):
        for j in range(17):
            lo = PAD + T * j
            b = B[p + 3, lo : lo + T]
            CY[p + 2, tile(j)] = 0.5 * (b + B[p + 3, lo - 1 : lo - 1 + T])
            if j < 16:
                zn = jnp.where(lane == 255, 0.0, pltpu.roll(b, 255, 1))
                zp = jnp.where(lane == 0, 0.0, pltpu.roll(b, 1, 1))
                CZP[p + 2, tile(j)] = 0.5 * (b + zn)
                CZM[p + 2, tile(j)] = 0.5 * (b + zp)

    def coef_x(p):
        for j in range(16):
            CX[p + 3, tile(j)] = 0.5 * (B[p + 3, padded(j)] + B[p + 4, padded(j)])

    loop(8, coef_yz)
    loop(7, coef_x)

    def lap(k, p, j):
        lo = PAD + T * j
        sl = tile(j)
        v = U[k, p + 3, lo : lo + T]
        t = CX[p + 3, sl] * (U[k, p + 4, lo : lo + T] - v) + CX[p + 2, sl] * (U[k, p + 2, lo : lo + T] - v)
        t = t + CY[p + 2, T * j + 1 : T * j + 1 + T] * (U[k, p + 3, lo + 1 : lo + 1 + T] - v)
        t = t + CY[p + 2, sl] * (U[k, p + 3, lo - 1 : lo - 1 + T] - v)
        zn = jnp.where(lane == 255, 0.0, pltpu.roll(v, 255, 1))
        zp = jnp.where(lane == 0, 0.0, pltpu.roll(v, 1, 1))
        return v, t + CZP[p + 2, sl] * (zn - v) + CZM[p + 2, sl] * (zp - v)

    def first_lap(p):
        for j in range(16):
            LU[0, p + 3, tile(j)] = lap(0, p, j)[1]

    loop(6, lambda i: first_lap(i + 1))

    d_l.wait()
    d_r.wait()
    near_d = jnp.concatenate([DH[0, 5:8], DS[...], DH[1, 0:3], jnp.zeros((2, 128), F32)], axis=0)
    rolled = [near_d if y == 0 else pltpu.roll(near_d, (-y) % 128, 1) for y in range(-3, 4)]
    key = jnp.transpose(jnp.concatenate(rolled + [jnp.zeros((16, 128), F32)], axis=0))
    for p in range(14):
        DB[p] = jnp.broadcast_to(key[:, 48 + p : 49 + p], (128, 128))
    idx = jnp.dot(key.astype(jnp.bfloat16), pick[...], preferred_element_type=F32) + shift[0:1, :]
    idx = jnp.clip(idx, 0.0, 255.0).astype(I32)
    for q in range(4):
        IDX[q] = idx[:, 128 * q : 128 * q + 128]
    SIDX[...] = idx[:, 512:640]
    RIDX[...] = idx[:, 640:768]

    def take(v, i):
        return jnp.take_along_axis(v, i, axis=1, mode="promise_in_bounds")

    def compact(which, read, spare=None):
        def body(t):
            halves = []
            for half in range(2):
                i = SIDX[pl.ds(pl.multiple_of(64 * half + T * t, T), T)]
                low, i = i < 128, i & 127
                for side in range(2):
                    for h in range(3):
                        v = read(7 - h if side else h, 64 * half + T * t)
                        g = jnp.where(low, take(v[:, :128], i), take(v[:, 128:], i))
                        start = 64 * side + STARTS[h]
                        out = g if start == 0 else jnp.where(lane1 >= start, g, out)
                    if spare is not None:
                        v = spare(6 if side else 1, 64 * half + T * t)
                        g = jnp.where(low, take(v[:, :128], i), take(v[:, 128:], i))
                        out = jnp.where(lane1 == 64 * side + SPARE, g, out)
                halves.append(out)
            a, b = halves
            SG[which, 0, t] = jnp.where(lane1 < 64, a, pltpu.roll(b, 64, 1))
            SG[which, 1, t] = jnp.where(lane1 < 64, pltpu.roll(a, 64, 1), b)

        loop(8, body)
        a = rcopy(SG.at[which, 0], RG.at[which, 1], hs.at[which, 0], hr.at[which, 0], left)
        b = rcopy(SG.at[which, 1], RG.at[which, 0], hs.at[which, 1], hr.at[which, 1], right)
        a.start()
        b.start()
        return a, b

    def at_ends(do):
        @pl.when(d == 0)
        def _():
            do(0)

        @pl.when(d == 31)
        def _():
            do(1)

    def expand(which, cps, write, heights):
        for cp in cps:
            cp.wait()

        def blank(side):
            for t in range(8):
                RG[which, side, t] = jnp.zeros((T, 128), F32)

        at_ends(blank)

        def body(t):
            for side in range(2):
                v = RG[which, side, t % 8]
                for h in heights:
                    i = INVH[3 * side + h, t]
                    g = jnp.concatenate([take(v, i[:, :128]), take(v, i[:, 128:])], axis=1)
                    write(8 + h if side else -1 - h, T * t, g)

        loop(16, body)

    def rows_at(first, n=T):
        return pl.ds(pl.multiple_of(first, T), n)

    h_b = compact(0, lambda p, y: B[p + 3, rows_at(PAD + y)])

    def invert_halo(t):
        cells = RIDX[rows_at(T * t)]
        for side in range(2):
            for h in range(3):
                inv = jnp.zeros((T, 256), I32)
                for j in range(STARTS[h], STARTS[h + 1]):
                    jj = 64 * side + j
                    inv = jnp.where(lane == cells[:, jj : jj + 1], j, inv)
                INVH[3 * side + h, t] = inv + 64 * (t // 8)

    loop(16, invert_halo)

    p_z.wait_recv()
    other = 2 * (1 - zl) + c
    p_f = rcopy(PG.at[other], PG.at[other], ps.at[2], pr.at[2], core)
    p_f.start()

    for cp in r_x:
        cp.wait()
    for k in range(4):
        sl = pl.ds(16 * k, 16)
        RY[k] = RX[gx, sl] + RX[4, sl] + RX[5, sl] + RX[6, sl]
    r_y = []
    for k in (1, 2, 3):
        cp = rcopy(RY.at[(gy + k) % 4], RY.at[3 + k], rs.at[2 + k], rr.at[2 + k], ys[k - 1])
        cp.start()
        r_y.append(cp)

    e_l.wait()
    e_r.wait()
    for e, p in enumerate((-1, 8)):
        for j in range(8):
            sl = slice(16 * j, 16 * j + 16)
            at = slice(PAD + 16 * j, PAD + 16 * j + 16)
            U[0, p + 3, at] = RE[e, 0, sl].astype(I32).astype(F32) * (1.0 / USCALE)
            B[p + 3, at] = RE[e, 1, sl].astype(I32).astype(F32) * (1.0 / BSCALE) + 1.0

    def no_edge(side):
        for j in range(16):
            U[0, 11 if side else 2, padded(j)] = zero
            B[11 if side else 2, padded(j)] = zero

    at_ends(no_edge)
    loop(2, lambda i: coef_x(8 * i - 1))
    loop(2, lambda i: first_lap(7 * i))
    ld_base.wait()
    ld_lat.wait()
    ld_sb.wait()
    p_c.wait()
    p_f.wait()
    p_z.wait_send()

    first = d * 8

    def step_one(p):
        factor = jnp.where(first + p == cell_x, wav[picked, 0], 0.0)
        for j in range(8):
            k, o = j // 2, (j % 2) * 16
            sl = slice(16 * j, 16 * j + 16)
            at = slice(PAD + 16 * j, PAD + 16 * j + 16)
            g = PG[k, 0, p, o : o + 16].astype(F32)
            b = PG[k, 1, p, o : o + 16].astype(F32)
            sq = jnp.tanh(LAT[p, sl] * g + b)
            m = BASE[p, sl] * jnp.exp(0.25 * sq)
            M[p + 3, sl] = m
            Q[p, sl] = m * 0.25 * (1.0 - sq * sq)
            U[1, p + 3, at] = 2.0 * U[0, p + 3, at] - SB[p, sl] + m * LU[0, p + 3, sl] + factor * HIT[sl]

    loop(6, lambda i: step_one(i + 2 * (i // 3)))
    h_u = compact(1, lambda p, y: U[1, p + 3, rows_at(PAD + y)], lambda p, y: U[0, p + 3, rows_at(PAD + y)])
    h_m = compact(2, lambda p, y: M[p + 3, rows_at(y)])
    loop(2, lambda i: step_one(i + 3))

    for cp in r_y:
        cp.wait()
    for k in range(2):
        sl = pl.ds(8 * k, 8)
        RZ[k] = RY[gy, sl] + RY[4, sl] + RY[5, sl] + RY[6, sl]
    r_z = rcopy(RZ.at[1 - gz], RZ.at[2], rs.at[6], rr.at[6], zs)
    r_z.start()

    def write_b(p, y, g):
        B[p + 3, rows_at(PAD + y)] = g

    expand(0, h_b, write_b, (1, 2))
    loop(2, lambda i: coef_yz(9 * i - 1))
    loop(2, lambda i: coef_yz(11 * i - 2))
    loop(2, lambda i: coef_x(10 * i - 2))
    loop(2, lambda i: coef_x(12 * i - 3))

    r_z.wait()
    RALL[s] = RZ[gz] + RZ[2]
    r_s = []
    for i, p in enumerate((core, zlo, far)):
        cp = rcopy(RALL.at[s], RALL.at[s], rs.at[7 + i], rr.at[7 + i], p)
        cp.start()
        r_s.append(cp)

    def step(n, p):
        factor = jnp.where(first + p == cell_x, wav[picked, n], 0.0)
        for j in range(16):
            sl = tile(j)
            v, a = lap(n, p, j)
            LU[n, p + 3, sl] = a
            new = 2.0 * v - U[n - 1, p + 3, padded(j)] + M[p + 3, sl] * a + factor * HIT[sl]
            U[n + 1, p + 3, padded(j)] = new
            AA[n, p + 3, sl] = jnp.where(lane_f == twice(DB[p + 3, sl]), new - twice(RB[n, p + 3, sl]), 0.0)

    def last_step(p):
        factor = jnp.where(first + p == cell_x, wav[picked, 3], 0.0)
        for j in range(16):
            sl = tile(j)
            v, a = lap(3, p, j)
            m = M[p + 3, sl]
            LU[3, p + 3, sl] = a
            new = 2.0 * v - U[2, p + 3, padded(j)] + m * a + factor * HIT[sl]
            r = jnp.where(lane_f == twice(DB[p + 3, sl]), new - twice(RB[3, p + 3, sl]), 0.0)
            AA[3, p + 3, sl] = r
            U[0, p + 3, padded(j)] = m * r

    for cp in r_s:
        cp.wait()
    rt = jnp.transpose(jnp.concatenate([RALL[k] for k in range(4)] + [jnp.zeros((96, 128), F32)], axis=0))
    for k in range(4):
        for x in range(8):
            RB[k, x + 3] = jnp.broadcast_to(rt[:, 8 * k + x : 8 * k + x + 1], (128, 128))

    def inside(t, _):
        loop(6 - 2 * t, lambda i: step(1 + t, 1 + t + i))
        return 0

    lax.fori_loop(0, 2, inside, 0)
    loop(2, lambda i: last_step(3 + i))

    def write_u(p, y, g):
        U[1, p + 3, rows_at(PAD + y)] = g

    def write_m(p, y, g):
        M[p + 3, rows_at(y)] = g

    expand(1, h_u, write_u, (0, 1, 2))

    def second(t):
        slot = jnp.full((T, 128), SPARE, I32) + 64 * (t // 8)
        for side in range(2):
            U[0, 12 if side else 1, rows_at(PAD + T * t)] = twice(take(RG[1, side, t % 8], slot))

    loop(16, second)
    expand(2, h_m, write_m, (0, 1, 2))

    def outside(t, _):
        loop(6, lambda i: step(1 + t, t - 2 + i + (6 - 2 * t) * (i // 3)))
        return 0

    lax.fori_loop(0, 2, outside, 0)
    loop(6, lambda i: last_step(i + 2 * (i // 3)))

    sends = [(3, 0), (3, 1), (3, 2), (2, 0), (2, 1), (1, 0)]

    def pack(t):
        at = rows_at(T * t)
        out = jnp.zeros((T, 128), F32)
        for side in range(2):
            for i, (k, h) in enumerate(sends):
                total = jnp.sum(AA[k, 3 + (7 - h if side else h), at], axis=1, keepdims=True)
                out = jnp.where(lane1 == 8 * side + i, total, out)
        KT[at] = out

    loop(16, pack)
    packed = jnp.transpose(KT[...])
    SR[0] = packed[0:8]
    SR[1] = packed[8:16]
    r_l = rcopy(SR.at[0], RR.at[1], ds_.at[2], dr_.at[2], left)
    r_r = rcopy(SR.at[1], RR.at[0], ds_.at[3], dr_.at[3], right)
    r_l.start()
    r_r.start()

    def back(k, p):
        for j in range(16):
            sl = tile(j)
            _, t = lap(3 - k, p, j)
            a = AA[k - 1, p + 3, sl] + t + 2.0 * AA[k, p + 3, sl] - AA[k + 1, p + 3, sl]
            AA[k - 1, p + 3, sl] = a
            U[4 - k, p + 3, padded(j)] = M[p + 3, sl] * a

    def finish(p):
        for j in range(16):
            sl = tile(j)
            _, t = lap(2, p, j)
            a2, a3 = AA[1, p + 3, sl], AA[2, p + 3, sl]
            a1 = AA[0, p + 3, sl] + t + 2.0 * a2 - a3
            img = AA[3, p + 3, sl] * LU[3, p + 3, sl] + a3 * LU[2, p + 3, sl]
            img = img + a2 * LU[1, p + 3, sl] + a1 * LU[0, p + 3, sl]
            IMG[p, sl] = img
            com = img * Q[p, sl]
            CB[p, sl] = com
            CA[p, sl] = com * LAT[p, sl]

    def resid_one(p):
        for j in range(16):
            sl = tile(j)
            r = U[1, p + 3, padded(j)] - twice(RB[0, p + 3, sl])
            AA[0, p + 3, sl] = jnp.where(lane_f == twice(DB[p + 3, sl]), r, 0.0)

    loop(8, resid_one)

    def inside_back(t, _):
        loop(6 - 2 * t, lambda i: back(3 - t, 1 + t + i))
        return 0

    lax.fori_loop(0, 2, inside_back, 0)
    loop(2, lambda i: finish(3 + i))

    def invert(t):
        at = rows_at(32 * s + T * t)
        for q in range(4):
            cells = IDX[q, at]
            for h in range(2):
                inv = jnp.full((T, 256), -1, I32)
                for j in range(63):
                    jj = 64 * h + j
                    inv = jnp.where(lane == cells[:, jj : jj + 1], jj, inv)
                INV[2 * q + h, t] = inv

    loop(4, invert)

    r_l.wait()
    r_r.wait()

    def no_resid(side):
        RR[side] = jnp.zeros((8, 128), F32)

    at_ends(no_resid)
    KT[...] = jnp.transpose(jnp.concatenate([RR[0], RR[1], jnp.zeros((112, 128), F32)], axis=0))
    for side in range(2):
        for i, (k, h) in enumerate(sends):
            p = 8 + h if side else -1 - h
            for j in range(16):
                sl = tile(j)
                col = 8 * side + i
                r = jnp.where(lane_f == twice(DB[p + 3, sl]), KT[sl, col : col + 1], 0.0)
                AA[k, p + 3, sl] = r
                if k == 3:
                    U[0, p + 3, padded(j)] = M[p + 3, sl] * r

    def outside_back(t, _):
        loop(6, lambda i: back(3 - t, t - 2 + i + (6 - 2 * t) * (i // 3)))
        return 0

    lax.fori_loop(0, 2, outside_back, 0)
    loop(6, lambda i: finish(i + 2 * (i // 3)))
    out_i = load(0, IMG, img_h)

    def compact_grads(k):
        def body(t):
            at = rows_at(32 * k + T * t)
            for q in range(4):
                i = IDX[q, at]
                low, i = i < 128, i & 127
                for f, src in enumerate((CA, CB)):
                    halves = []
                    for x in (2 * q, 2 * q + 1):
                        v = src[x, at]
                        halves.append(jnp.where(low, take(v[:, :128], i), take(v[:, 128:], i)))
                    CG[k, f, q, t] = jnp.where(lane1 < 64, halves[0], halves[1])

        loop(4, body)

    g_c = []
    for i in (1 - zl, zl):
        compact_grads(2 * i + (1 - c))
        cp = rcopy(CG.at[2 * i + (1 - c)], RA.at[i], gs.at[i], gr.at[i], core)
        cp.start()
        g_c.append(cp)
    pair = 2 * (1 - zl) + c
    compact_grads(pair)
    g_c[0].wait()
    for f in range(2):
        for q in range(4):
            CG[pair, f, q] = CG[pair, f, q] + RA[1 - zl, f, q]
    g_z = rcopy(CG.at[pair], RBUF, gs.at[2], gr.at[2], zlo)
    g_z.start()
    g_c[1].wait()
    g_z.wait()

    def spread(t):
        at, to = rows_at(32 * s + T * t), rows_at(T * t)
        for q in range(4):
            for f, src, out in ((0, CA, GA), (1, CB, GB)):
                v = RA[zl, f, q, t] + RBUF[f, q, t]
                for x in (2 * q, 2 * q + 1):
                    i = INV[x, t]
                    have, i = i >= 0, i & 127
                    g = jnp.concatenate([take(v, i[:, :128]), take(v, i[:, 128:])], axis=1)
                    out[x, to] = src[x, at] + jnp.where(have, g, 0.0)

    loop(4, spread)
    out_g = load(1, GA, gg_h)
    out_b = load(2, GB, bg_h)
    out_i.wait()
    out_g.wait()
    out_b.wait()


def shards(
    state_before, state_now, base_model, buoyancy, latent, flow_gain, flow_bias, records, source_wavelet, source_cell,
    shot, receiver_depth,
):
    any_ = pl.BlockSpec(memory_space=pl.ANY)
    smem = pl.BlockSpec(memory_space=pltpu.SMEM)
    vmem = pl.BlockSpec(memory_space=pltpu.VMEM)
    field = (8, 128, 256)
    halo = (14, 144, 256)
    pick, shift = tables()
    img, gg, bg = pl.pallas_call(
        kernel,
        out_shape=(
            jax.ShapeDtypeStruct(field, F32),
            jax.ShapeDtypeStruct((8, 32, 256), F32),
            jax.ShapeDtypeStruct((8, 32, 256), F32),
        ),
        in_specs=[any_] * 8 + [smem] * 3 + [vmem] * 3,
        out_specs=(any_, any_, any_),
        scratch_shapes=[
            pltpu.VMEM((4,) + halo, F32),
            pltpu.VMEM(halo, F32),
            pltpu.VMEM(field, F32),
            pltpu.VMEM(field, F32),
            pltpu.VMEM(field, F32),
            pltpu.VMEM((4, 2, 8, 32, 256), jnp.bfloat16),
            pltpu.VMEM((2, 256, 128), jnp.bfloat16),
            pltpu.VMEM((4, 14, 128, 256), F32),
            pltpu.VMEM((5, 14, 128, 256), F32),
            pltpu.VMEM((14, 128, 256), F32),
            pltpu.VMEM(field, F32),
            pltpu.VMEM((13, 128, 256), F32),
            pltpu.VMEM((12, 136, 256), F32),
            pltpu.VMEM((12, 128, 256), F32),
            pltpu.VMEM((12, 128, 256), F32),
            pltpu.VMEM((14, 128, 128), F32),
            pltpu.VMEM((4, 14, 128, 128), F32),
            pltpu.VMEM((128, 256), F32),
            pltpu.VMEM(field, F32),
            pltpu.VMEM(field, F32),
            pltpu.VMEM(field, F32),
            pltpu.VMEM((8, 32, 256), F32),
            pltpu.VMEM((8, 32, 256), F32),
            pltpu.VMEM((4, 2, 4, 4, 8, 128), F32),
            pltpu.VMEM((2, 2, 4, 4, 8, 128), F32),
            pltpu.VMEM((2, 4, 4, 8, 128), F32),
            pltpu.VMEM((7, 64, 128), F32),
            pltpu.VMEM((7, 16, 128), F32),
            pltpu.VMEM((3, 8, 128), F32),
            pltpu.VMEM((4, 8, 128), F32),
            pltpu.VMEM((8, 128), F32),
            pltpu.VMEM((2, 8, 128), F32),
            pltpu.VMEM((4, 128, 128), I32),
            pltpu.VMEM((8, 4, 8, 256), I32),
            pltpu.VMEM((128, 128), I32),
            pltpu.VMEM((128, 128), I32),
            pltpu.VMEM((6, 16, 8, 256), I32),
            pltpu.VMEM((2, 2, 128, 256), jnp.int16),
            pltpu.VMEM((2, 2, 128, 256), jnp.int16),
            pltpu.VMEM((3, 2, 8, 8, 128), F32),
            pltpu.VMEM((3, 2, 8, 8, 128), F32),
            pltpu.VMEM((128, 128), F32),
            pltpu.VMEM((2, 8, 128), F32),
            pltpu.VMEM((2, 8, 128), F32),
            pltpu.SemaphoreType.DMA((8,)),
            pltpu.SemaphoreType.DMA((2,)),
            pltpu.SemaphoreType.DMA((2,)),
            pltpu.SemaphoreType.DMA((3, 2)),
            pltpu.SemaphoreType.DMA((3, 2)),
            pltpu.SemaphoreType.DMA((3,)),
            pltpu.SemaphoreType.DMA((3,)),
            pltpu.SemaphoreType.DMA((3,)),
            pltpu.SemaphoreType.DMA((3,)),
            pltpu.SemaphoreType.DMA((10,)),
            pltpu.SemaphoreType.DMA((10,)),
            pltpu.SemaphoreType.DMA((4,)),
            pltpu.SemaphoreType.DMA((4,)),
        ],
        compiler_params=pltpu.CompilerParams(
            collective_id=1, has_side_effects=True, vmem_limit_bytes=58 << 20
        ),
        name="flow_gradient",
    )(
        state_before[0], state_now[0], base_model, buoyancy, latent[0], flow_gain, flow_bias, records, source_wavelet,
        source_cell, shot, receiver_depth, jnp.asarray(pick, jnp.bfloat16), jnp.asarray(shift),
    )
    return img[None], gg, bg


def solution(mesh):
    in_specs = (
        P("smp", "dom", None, None),
        P("smp", "dom", None, None),
        P("dom", None, None),
        P("dom", None, None),
        P("smp", "dom", None, None),
        P("dom", "smp", None),
        P("dom", "smp", None),
        P("dom", None, None, None),
        P(),
        P(),
        P(),
        P("dom", None),
    )
    out_specs = (P("smp", "dom", None, None), P("dom", "smp", None), P("dom", "smp", None))
    return jax.shard_map(shards, mesh=mesh, in_specs=in_specs, out_specs=out_specs, check_vma=False)
```

time: 107 us -> 72.2 us (0.67)
  Pallas kernels: 98.8 us -> 64.6 us
    pallas_call x1, Pallas kernels: 98.8 us -> 64.6 us  [shards(): pl.pallas_call(kernel, out_shape=(jax.ShapeDtypeStruct(field, F32), jax.S...]
where the time goes in v3:
time: 72.2 us; the launch traced here: 71.4 us
  Pallas kernels  64.6 us (89%)
  local copies, waits for them, and re-layouts  5.44 us (8%)
  between operations  1.3 us (2%)
    pallas_call x1, Pallas kernels, shards(): pl.pallas_call(kernel, out_shape=(jax.ShapeDtypeStruct(field, F32), jax.S...  64.6 us
    unnamed x10, local copies, waits for them, and re-layouts  5.44 us

profile of v3, /device:TPU:1, one launch (start us, length us, event | category | flops | bytes accessed | tf_op | source)
XLA Modules:
  0.0 71.4 jit_solution(3252325513036020041)
XLA Ops:
  1.3 0.0 copy-start.2
  1.3 0.7 copy-done.2
  2.0 0.7 copy.17.wav
  2.7 64.6 %flow_gradient.1 = (f32[8,128,256]{2,1,0:T(8,128)}, f32[8,32,256]{2,1,0:T(8,128)}, f32[8,32,256]{2,1,0:T(8,128)}) custom-call(f32[8,128,256]{2,1,0:T(8,128)} %bitcast.5, f32[8,128,256]{2,1,0:T(8,128)} %bitcast.6, f32[8,128,256]{2,1,0:T(8,128)} %base_h.1, f32[8,128,256]{2,1,0:T(8,128)} %buoy_h.1, f32[8,128,256]{2,1,0:T(8,128)} %bitcast.7, ...), custom_call_target="tpu_custom_call" | custom-call | tf_op jit(solution)/shard_map/flow_gradient/pallas_call | solution.py:613
  67.3 0.0 copy-start.1
  67.3 2.3 %copy.22 = f32[1,8,128,256]{3,2,1,0:T(8,128)} copy(f32[1,8,128,256]{3,2,1,0:T(8,128)} %bitcast.4) | data formatting | bytes 2097152
  69.6 0.0 copy-done.1
  69.6 0.0 copy-start
  69.6 0.7 copy.23
  70.3 0.3 copy-done
  70.7 0.7 copy.24
Async XLA Ops:
  1.3 0.7 copy-start.2
  67.3 2.3 %copy-start.1 = (f32[8,32,256]{2,1,0:T(8,128)S(1)}, f32[8,32,256]{2,1,0:T(8,128)}, u32[]{:S(2)}) copy-start(f32[8,32,256]{2,1,0:T(8,128)} %get-tuple-element.13) | copy-start | bytes 786436
  69.6 1.0 %copy-start = (f32[8,32,256]{2,1,0:T(8,128)S(1)}, f32[8,32,256]{2,1,0:T(8,128)}, u32[]{:S(2)}) copy-start(f32[8,32,256]{2,1,0:T(8,128)} %get-tuple-element.14) | copy-start | bytes 786436

commit v4 on v3

--- a/solution.py
+++ b/solution.py
@@ -34,16 +34,24 @@
 BSCALE = 65532.0
 
 
+def bands(cells, base=0):
+    out = {}
+    for i, (p, y, z) in enumerate(cells):
+        w, first = out.get((p, y), (0, base + i))
+        out[p, y] = (max(w, abs(z)), first)
+    return out
+
+
 def tables():
     up = sum((across(h) for h in (1, 2, 3)), [])
     down = [(-1 - p, y, z) for p, y, z in up]
     right = [[(p + 8, y, z) for p, y, z in cells] for cells in (up, down)]
-    lists = [near(x) for x in range(8)] + [down, right[0], up, right[1]]
+    lists = [near(x) for x in range(8)] + [down, right[0]]
     pick = np.zeros((128, 64 * len(lists)), np.float32)
     shift = np.zeros((8, 64 * len(lists)), np.float32)
     for i, cells in enumerate(lists):
         if i >= 8:
-            cells = cells + [{8: (-1, 0, 0), 9: (8, 0, 0), 10: (0, 0, 0), 11: (7, 0, 0)}[i]]
+            cells = cells + [{8: (-1, 0, 0), 9: (8, 0, 0)}[i]]
         cells = cells + [cells[0]] * (64 - len(cells))
         for j, (p, y, z) in enumerate(cells):
             pick[16 * (y + 3) + p + 3, 64 * i + j] = 1.0
@@ -54,13 +62,14 @@
 F32 = jnp.float32
 PAD = 8
 T = 8
+G = 128
 
 
 def kernel(
     sb_h, sn_h, base_h, buoy_h, lat_h, gain_h, bias_h, rec_h, wav, cell, shot, depth, pick, shift,
     img_h, gg_h, bg_h,
-    U, B, SB, BASE, LAT, PG, RQ, LU, AA, M, Q, CX, CY, CZP, CZM, DB, RB, HIT, IMG, CA, CB, GA, GB, CG, RA, RBUF,
-    RX, RY, RZ, RALL, DS, DH, IDX, INV, SIDX, RIDX, INVH, SE, RE, SG, RG, KT, SR, RR,
+    U, B, SB, BASE, LAT, PG, RQ, LU, AA, M, Q, CX, CYP, CYM, CZP, CZM, DG, DB, RB, KEY, HIT, IMG, CA, CB, GA, GB, CG, RA, RBUF,
+    RX, RY, RZ, RALL, DS, DH, IDX, INV, SIDX, INVH, SE, RE, SG, RG, KT, SR, RR,
     lsem, es, er, hs, hr, ps, pr, gs, gr, rs, rr, ds_, dr_,
 ):
     d = lax.axis_index("dom")
@@ -101,17 +110,27 @@
             src_ref=src, dst_ref=dst, send_sem=ss, recv_sem=sr, device_id=dev, device_id_type=MESH
         )
 
-    def loop(n, body):
+    def loop(n, body, per=1):
         def run(i, _):
-            body(i)
+            for k in range(per):
+                body(i * per + k if per > 1 else i)
             return 0
 
-        lax.fori_loop(0, n, run, 0)
+        lax.fori_loop(0, n // per, run, 0)
+
+    def rows_at(first, n=T):
+        if isinstance(first, int):
+            return slice(first, first + n)
+        return pl.ds(pl.multiple_of(first, T), n)
+
+    def planes(n, body):
+        loop(n, lambda i: body(i, 0))
 
     zero = jnp.zeros((T, 256), F32)
     lane = lax.broadcasted_iota(I32, (T, 256), 1)
     lane1 = lax.broadcasted_iota(I32, (T, 128), 1)
     lane_f = lane.astype(F32)
+    sub = lax.broadcasted_iota(I32, (T, 256), 0)
 
     def tile(j):
         return slice(T * j, T * j + T)
@@ -138,7 +157,6 @@
     cell_x = flat // (128 * 256)
     cell_y = (flat // 256) % 128
     cell_z = flat % 256
-    sub = lax.broadcasted_iota(I32, (T, 256), 0)
     for j in range(16):
         HIT[tile(j)] = jnp.where((sub + T * j == cell_y) & (lane == cell_z), 1.0, 0.0)
     DS[...] = depth[...].astype(F32)
@@ -182,40 +200,43 @@
         cp.start()
         r_x.append(cp)
 
-    def coef_yz(p):
-        for j in range(17):
-            lo = PAD + T * j
-            b = B[p + 3, lo : lo + T]
-            CY[p + 2, tile(j)] = 0.5 * (b + B[p + 3, lo - 1 : lo - 1 + T])
-            if j < 16:
-                zn = jnp.where(lane == 255, 0.0, pltpu.roll(b, 255, 1))
-                zp = jnp.where(lane == 0, 0.0, pltpu.roll(b, 1, 1))
-                CZP[p + 2, tile(j)] = 0.5 * (b + zn)
-                CZM[p + 2, tile(j)] = 0.5 * (b + zp)
-
-    def coef_x(p):
-        for j in range(16):
-            CX[p + 3, tile(j)] = 0.5 * (B[p + 3, padded(j)] + B[p + 4, padded(j)])
-
-    loop(8, coef_yz)
-    loop(7, coef_x)
-
-    def lap(k, p, j):
-        lo = PAD + T * j
-        sl = tile(j)
-        v = U[k, p + 3, lo : lo + T]
-        t = CX[p + 3, sl] * (U[k, p + 4, lo : lo + T] - v) + CX[p + 2, sl] * (U[k, p + 2, lo : lo + T] - v)
-        t = t + CY[p + 2, T * j + 1 : T * j + 1 + T] * (U[k, p + 3, lo + 1 : lo + 1 + T] - v)
-        t = t + CY[p + 2, sl] * (U[k, p + 3, lo - 1 : lo - 1 + T] - v)
-        zn = jnp.where(lane == 255, 0.0, pltpu.roll(v, 255, 1))
-        zp = jnp.where(lane == 0, 0.0, pltpu.roll(v, 1, 1))
-        return v, t + CZP[p + 2, sl] * (zn - v) + CZM[p + 2, sl] * (zp - v)
-
-    def first_lap(p):
-        for j in range(16):
-            LU[0, p + 3, tile(j)] = lap(0, p, j)[1]
-
-    loop(6, lambda i: first_lap(i + 1))
+    def shifted(ref, at, y):
+        t = [ref[at + (rows_at(PAD + y - T),)], ref[at + (rows_at(PAD + y),)]]
+        for i in range(1, G // T + 1):
+            t.append(ref[at + (rows_at(PAD + y + T * i),)])
+            after = pltpu.roll(jnp.where(sub == 0, t[i + 1], t[i]), T - 1, 0)
+            before = pltpu.roll(jnp.where(sub == T - 1, t[i - 1], t[i]), 1, 0)
+            yield t[i], after, before
+
+    def coef(p, y):
+        for i, (b, after, before) in enumerate(shifted(B, (p + 3,), y)):
+            sl, at = rows_at(y + T * i), rows_at(PAD + y + T * i)
+            xp, xm = B[p + 4, at], B[p + 2, at]
+            zn = jnp.where(lane == 255, 0.0, pltpu.roll(b, 255, 1))
+            zp = jnp.where(lane == 0, 0.0, pltpu.roll(b, 1, 1))
+            CX[p + 3, sl] = 0.5 * (b + xp)
+            CX[p + 2, sl] = 0.5 * (b + xm)
+            CYP[p + 2, sl] = 0.5 * (b + after)
+            CYM[p + 2, sl] = 0.5 * (b + before)
+            CZP[p + 2, sl] = jnp.where(lane == 255, 0.0, 0.5 * (b + zn))
+            CZM[p + 2, sl] = jnp.where(lane == 0, 0.0, 0.5 * (b + zp))
+            DG[p + 2, sl] = 3.0 * b + 0.5 * ((xp + xm) + (after + before) + (zn + zp))
+
+    planes(6, lambda i, y: coef(i + 1, y))
+
+    def laps(k, p, y):
+        for i, (v, after, before) in enumerate(shifted(U, (k, p + 3), y)):
+            sl, at = rows_at(y + T * i), rows_at(PAD + y + T * i)
+            t = CX[p + 3, sl] * U[k, p + 4, at] + CX[p + 2, sl] * U[k, p + 2, at]
+            t = t + (CYP[p + 2, sl] * after + CYM[p + 2, sl] * before)
+            t = t + (CZP[p + 2, sl] * pltpu.roll(v, 255, 1) + CZM[p + 2, sl] * pltpu.roll(v, 1, 1))
+            yield sl, at, v, t - DG[p + 2, sl] * v
+
+    def first_lap(p, y):
+        for sl, _, _, t in laps(0, p, y):
+            LU[0, p + 3, sl] = t
+
+    planes(6, lambda i, y: first_lap(i + 1, y))
 
     d_l.wait()
     d_r.wait()
@@ -224,28 +245,28 @@
     key = jnp.transpose(jnp.concatenate(rolled + [jnp.zeros((16, 128), F32)], axis=0))
     for p in range(14):
         DB[p] = jnp.broadcast_to(key[:, 48 + p : 49 + p], (128, 128))
+    KEY[...] = key
     idx = jnp.dot(key.astype(jnp.bfloat16), pick[...], preferred_element_type=F32) + shift[0:1, :]
     idx = jnp.clip(idx, 0.0, 255.0).astype(I32)
     for q in range(4):
         IDX[q] = idx[:, 128 * q : 128 * q + 128]
     SIDX[...] = idx[:, 512:640]
-    RIDX[...] = idx[:, 640:768]
 
     def take(v, i):
         return jnp.take_along_axis(v, i, axis=1, mode="promise_in_bounds")
 
-    def compact(which, read, spare=None):
+    def compact(which, read, heights, spare=None):
         def body(t):
             halves = []
             for half in range(2):
                 i = SIDX[pl.ds(pl.multiple_of(64 * half + T * t, T), T)]
                 low, i = i < 128, i & 127
                 for side in range(2):
-                    for h in range(3):
+                    for h in heights:
                         v = read(7 - h if side else h, 64 * half + T * t)
                         g = jnp.where(low, take(v[:, :128], i), take(v[:, 128:], i))
                         start = 64 * side + STARTS[h]
-                        out = g if start == 0 else jnp.where(lane1 >= start, g, out)
+                        out = g if side == 0 and h == heights[0] else jnp.where(lane1 >= start, g, out)
                     if spare is not None:
                         v = spare(6 if side else 1, 64 * half + T * t)
                         g = jnp.where(low, take(v[:, :128], i), take(v[:, 128:], i))
@@ -255,7 +276,7 @@
             SG[which, 0, t] = jnp.where(lane1 < 64, a, pltpu.roll(b, 64, 1))
             SG[which, 1, t] = jnp.where(lane1 < 64, pltpu.roll(a, 64, 1), b)
 
-        loop(8, body)
+        loop(8, body, 4)
         a = rcopy(SG.at[which, 0], RG.at[which, 1], hs.at[which, 0], hr.at[which, 0], left)
         b = rcopy(SG.at[which, 1], RG.at[which, 0], hs.at[which, 1], hr.at[which, 1], right)
         a.start()
@@ -289,24 +310,43 @@
                     g = jnp.concatenate([take(v, i[:, :128]), take(v, i[:, 128:])], axis=1)
                     write(8 + h if side else -1 - h, T * t, g)
 
-        loop(16, body)
-
-    def rows_at(first, n=T):
-        return pl.ds(pl.multiple_of(first, T), n)
-
-    h_b = compact(0, lambda p, y: B[p + 3, rows_at(PAD + y)])
+        loop(16, body, 4)
+
+    h_b = compact(
+        0, lambda p, y: B[p + 3, rows_at(PAD + y)], (1, 2), lambda p, y: U[0, p + 3, rows_at(PAD + y)]
+    )
+
+    ups = [bands(across(h + 1), STARTS[h]) for h in range(3)]
+    downs = [{(7 - p, y): v for (p, y), v in band.items()} for band in ups]
+
+    def mark(invs, maps, cells):
+        for p, y in sorted(set().union(*maps)):
+            col = 16 * (y + 3) + p + 3
+            off = lane_f - cells[:, col : col + 1]
+            dist = jnp.abs(off)
+            for i, band in enumerate(maps):
+                if (p, y) in band:
+                    w, base = band[p, y]
+                    invs[i] = jnp.where(dist <= w, off + (base + w), invs[i])
+        return invs
 
     def invert_halo(t):
-        cells = RIDX[rows_at(T * t)]
-        for side in range(2):
+        cells = KEY[rows_at(T * t)]
+        for side, maps in enumerate((ups, downs)):
+            invs = mark([jnp.zeros((T, 256), F32)] * 3, maps, cells)
             for h in range(3):
-                inv = jnp.zeros((T, 256), I32)
-                for j in range(STARTS[h], STARTS[h + 1]):
-                    jj = 64 * side + j
-                    inv = jnp.where(lane == cells[:, jj : jj + 1], j, inv)
-                INVH[3 * side + h, t] = inv + 64 * (t // 8)
-
-    loop(16, invert_halo)
+                INVH[3 * side + h, t] = invs[h].astype(I32) + 64 * (t // 8)
+
+    loop(16, invert_halo, 2)
+
+    def invert(t):
+        cells = KEY[rows_at(32 * s + T * t)]
+        maps = [bands(near(x), 64 * (x % 2)) for x in range(8)]
+        invs = mark([jnp.full((T, 256), -1.0, F32)] * 8, maps, cells)
+        for x in range(8):
+            INV[x, t] = invs[x].astype(I32)
+
+    loop(4, invert)
 
     p_z.wait_recv()
     other = 2 * (1 - zl) + c
@@ -339,8 +379,8 @@
             B[11 if side else 2, padded(j)] = zero
 
     at_ends(no_edge)
-    loop(2, lambda i: coef_x(8 * i - 1))
-    loop(2, lambda i: first_lap(7 * i))
+    planes(2, lambda i, y: coef(7 * i, y))
+    planes(2, lambda i, y: first_lap(7 * i, y))
     ld_base.wait()
     ld_lat.wait()
     ld_sb.wait()
@@ -350,24 +390,27 @@
 
     first = d * 8
 
-    def step_one(p):
-        factor = jnp.where(first + p == cell_x, wav[picked, 0], 0.0)
-        for j in range(8):
-            k, o = j // 2, (j % 2) * 16
-            sl = slice(16 * j, 16 * j + 16)
-            at = slice(PAD + 16 * j, PAD + 16 * j + 16)
-            g = PG[k, 0, p, o : o + 16].astype(F32)
-            b = PG[k, 1, p, o : o + 16].astype(F32)
+    def pulse(n, p):
+        return jnp.where(first + p == cell_x, wav[n, picked], 0.0)
+
+    def step_one(p, y):
+        factor = pulse(0, p)
+        for i in range(G // 16):
+            sl, at = rows_at(y + 16 * i, 16), rows_at(PAD + y + 16 * i, 16)
+            k, o = i // 2, slice(16 * (i % 2), 16 * (i % 2) + 16)
+            g = PG[k, 0, p, o].astype(F32)
+            b = PG[k, 1, p, o].astype(F32)
             sq = jnp.tanh(LAT[p, sl] * g + b)
             m = BASE[p, sl] * jnp.exp(0.25 * sq)
             M[p + 3, sl] = m
             Q[p, sl] = m * 0.25 * (1.0 - sq * sq)
-            U[1, p + 3, at] = 2.0 * U[0, p + 3, at] - SB[p, sl] + m * LU[0, p + 3, sl] + factor * HIT[sl]
-
-    loop(6, lambda i: step_one(i + 2 * (i // 3)))
-    h_u = compact(1, lambda p, y: U[1, p + 3, rows_at(PAD + y)], lambda p, y: U[0, p + 3, rows_at(PAD + y)])
-    h_m = compact(2, lambda p, y: M[p + 3, rows_at(y)])
-    loop(2, lambda i: step_one(i + 3))
+            new = 2.0 * U[0, p + 3, at] - SB[p, sl] + m * LU[0, p + 3, sl]
+            U[1, p + 3, at] = new + factor * HIT[sl]
+
+    planes(6, lambda i, y: step_one(i + 2 * (i // 3), y))
+    h_u = compact(1, lambda p, y: U[1, p + 3, rows_at(PAD + y)], (0, 1, 2))
+    h_m = compact(2, lambda p, y: M[p + 3, rows_at(y)], (0, 1, 2))
+    planes(2, lambda i, y: step_one(i + 3, y))
 
     for cp in r_y:
         cp.wait()
@@ -381,10 +424,14 @@
         B[p + 3, rows_at(PAD + y)] = g
 
     expand(0, h_b, write_b, (1, 2))
-    loop(2, lambda i: coef_yz(9 * i - 1))
-    loop(2, lambda i: coef_yz(11 * i - 2))
-    loop(2, lambda i: coef_x(10 * i - 2))
-    loop(2, lambda i: coef_x(12 * i - 3))
+
+    def second(t):
+        slot = jnp.full((T, 128), SPARE, I32) + 64 * (t // 8)
+        for side in range(2):
+            U[0, 12 if side else 1, rows_at(PAD + T * t)] = twice(take(RG[0, side, t % 8], slot))
+
+    loop(16, second, 4)
+    planes(4, lambda i, y: coef(i - 2 + 8 * (i // 2), y))
 
     r_z.wait()
     RALL[s] = RZ[gz] + RZ[2]
@@ -394,27 +441,23 @@
         cp.start()
         r_s.append(cp)
 
-    def step(n, p):
-        factor = jnp.where(first + p == cell_x, wav[picked, n], 0.0)
-        for j in range(16):
-            sl = tile(j)
-            v, a = lap(n, p, j)
+    def advance(n, p):
+        factor = pulse(n, p)
+        for sl, at, v, a in laps(n, p, 0):
+            m = M[p + 3, sl]
             LU[n, p + 3, sl] = a
-            new = 2.0 * v - U[n - 1, p + 3, padded(j)] + M[p + 3, sl] * a + factor * HIT[sl]
-            U[n + 1, p + 3, padded(j)] = new
-            AA[n, p + 3, sl] = jnp.where(lane_f == twice(DB[p + 3, sl]), new - twice(RB[n, p + 3, sl]), 0.0)
-
-    def last_step(p):
-        factor = jnp.where(first + p == cell_x, wav[picked, 3], 0.0)
-        for j in range(16):
-            sl = tile(j)
-            v, a = lap(3, p, j)
-            m = M[p + 3, sl]
-            LU[3, p + 3, sl] = a
-            new = 2.0 * v - U[2, p + 3, padded(j)] + m * a + factor * HIT[sl]
-            r = jnp.where(lane_f == twice(DB[p + 3, sl]), new - twice(RB[3, p + 3, sl]), 0.0)
-            AA[3, p + 3, sl] = r
-            U[0, p + 3, padded(j)] = m * r
+            new = 2.0 * v - U[n - 1, p + 3, at] + m * a + factor * HIT[sl]
+            r = jnp.where(lane_f == twice(DB[p + 3, sl]), new - twice(RB[n, p + 3, sl]), 0.0)
+            AA[n, p + 3, sl] = r
+            yield sl, at, m, new, r
+
+    def step(n, p, y):
+        for _, at, _, new, _ in advance(n, p):
+            U[n + 1, p + 3, at] = new
+
+    def last_step(p, y):
+        for _, at, m, _, r in advance(3, p):
+            U[0, p + 3, at] = m * r
 
     for cp in r_s:
         cp.wait()
@@ -424,11 +467,11 @@
             RB[k, x + 3] = jnp.broadcast_to(rt[:, 8 * k + x : 8 * k + x + 1], (128, 128))
 
     def inside(t, _):
-        loop(6 - 2 * t, lambda i: step(1 + t, 1 + t + i))
+        planes(6 - 2 * t, lambda i, y: step(1 + t, 1 + t + i, y))
         return 0
 
     lax.fori_loop(0, 2, inside, 0)
-    loop(2, lambda i: last_step(3 + i))
+    planes(2, lambda i, y: last_step(3 + i, y))
 
     def write_u(p, y, g):
         U[1, p + 3, rows_at(PAD + y)] = g
@@ -438,20 +481,14 @@
 
     expand(1, h_u, write_u, (0, 1, 2))
 
-    def second(t):
-        slot = jnp.full((T, 128), SPARE, I32) + 64 * (t // 8)
-        for side in range(2):
-            U[0, 12 if side else 1, rows_at(PAD + T * t)] = twice(take(RG[1, side, t % 8], slot))
-
-    loop(16, second)
     expand(2, h_m, write_m, (0, 1, 2))
 
     def outside(t, _):
-        loop(6, lambda i: step(1 + t, t - 2 + i + (6 - 2 * t) * (i // 3)))
+        planes(6, lambda i, y: step(1 + t, t - 2 + i + (6 - 2 * t) * (i // 3), y))
         return 0
 
     lax.fori_loop(0, 2, outside, 0)
-    loop(6, lambda i: last_step(i + 2 * (i // 3)))
+    planes(6, lambda i, y: last_step(i + 2 * (i // 3), y))
 
     sends = [(3, 0), (3, 1), (3, 2), (2, 0), (2, 1), (1, 0)]
 
@@ -464,7 +501,7 @@
                 out = jnp.where(lane1 == 8 * side + i, total, out)
         KT[at] = out
 
-    loop(16, pack)
+    loop(16, pack, 4)
     packed = jnp.transpose(KT[...])
     SR[0] = packed[0:8]
     SR[1] = packed[8:16]
@@ -473,18 +510,14 @@
     r_l.start()
     r_r.start()
 
-    def back(k, p):
-        for j in range(16):
-            sl = tile(j)
-            _, t = lap(3 - k, p, j)
+    def back(k, p, y):
+        for sl, at, _, t in laps(3 - k, p, y):
             a = AA[k - 1, p + 3, sl] + t + 2.0 * AA[k, p + 3, sl] - AA[k + 1, p + 3, sl]
             AA[k - 1, p + 3, sl] = a
-            U[4 - k, p + 3, padded(j)] = M[p + 3, sl] * a
-
-    def finish(p):
-        for j in range(16):
-            sl = tile(j)
-            _, t = lap(2, p, j)
+            U[4 - k, p + 3, at] = M[p + 3, sl] * a
+
+    def finish(p, y):
+        for sl, at, _, t in laps(2, p, y):
             a2, a3 = AA[1, p + 3, sl], AA[2, p + 3, sl]
             a1 = AA[0, p + 3, sl] + t + 2.0 * a2 - a3
             img = AA[3, p + 3, sl] * LU[3, p + 3, sl] + a3 * LU[2, p + 3, sl]
@@ -494,33 +527,20 @@
             CB[p, sl] = com
             CA[p, sl] = com * LAT[p, sl]
 
-    def resid_one(p):
-        for j in range(16):
-            sl = tile(j)
-            r = U[1, p + 3, padded(j)] - twice(RB[0, p + 3, sl])
+    def resid_one(p, y):
+        for i in range(G // T):
+            sl = rows_at(y + T * i)
+            r = U[1, p + 3, rows_at(PAD + y + T * i)] - twice(RB[0, p + 3, sl])
             AA[0, p + 3, sl] = jnp.where(lane_f == twice(DB[p + 3, sl]), r, 0.0)
 
-    loop(8, resid_one)
+    planes(8, resid_one)
 
     def inside_back(t, _):
-        loop(6 - 2 * t, lambda i: back(3 - t, 1 + t + i))
+        planes(6 - 2 * t, lambda i, y: back(3 - t, 1 + t + i, y))
         return 0
 
     lax.fori_loop(0, 2, inside_back, 0)
-    loop(2, lambda i: finish(3 + i))
-
-    def invert(t):
-        at = rows_at(32 * s + T * t)
-        for q in range(4):
-            cells = IDX[q, at]
-            for h in range(2):
-                inv = jnp.full((T, 256), -1, I32)
-                for j in range(63):
-                    jj = 64 * h + j
-                    inv = jnp.where(lane == cells[:, jj : jj + 1], jj, inv)
-                INV[2 * q + h, t] = inv
-
-    loop(4, invert)
+    planes(2, lambda i, y: finish(3 + i, y))
 
     r_l.wait()
     r_r.wait()
@@ -542,11 +562,11 @@
                     U[0, p + 3, padded(j)] = M[p + 3, sl] * r
 
     def outside_back(t, _):
-        loop(6, lambda i: back(3 - t, t - 2 + i + (6 - 2 * t) * (i // 3)))
+        planes(6, lambda i, y: back(3 - t, t - 2 + i + (6 - 2 * t) * (i // 3), y))
         return 0
 
     lax.fori_loop(0, 2, outside_back, 0)
-    loop(6, lambda i: finish(i + 2 * (i // 3)))
+    planes(6, lambda i, y: finish(i + 2 * (i // 3), y))
     out_i = load(0, IMG, img_h)
 
     def compact_grads(k):
@@ -600,6 +620,19 @@
     out_b.wait()
 
 
+def hand_out(img, gg, bg, img_o, gg_o, bg_o, vi, vg, vb, sem):
+    moves = [(img.at[p], vi.at[p], img_o.at[p]) for p in range(8)] + [(gg, vg, gg_o), (bg, vb, bg_o)]
+    come = [pltpu.make_async_copy(a, b, sem.at[0, i]) for i, (a, b, _) in enumerate(moves)]
+    go = [pltpu.make_async_copy(b, o, sem.at[1, i]) for i, (_, b, o) in enumerate(moves)]
+    for cp in come:
+        cp.start()
+    for a, b in zip(come, go):
+        a.wait()
+        b.start()
+    for cp in go:
+        cp.wait()
+
+
 def shards(
     state_before, state_now, base_model, buoyancy, latent, flow_gain, flow_bias, records, source_wavelet, source_cell,
     shot, receiver_depth,
@@ -610,13 +643,14 @@
     field = (8, 128, 256)
     halo = (14, 144, 256)
     pick, shift = tables()
-    img, gg, bg = pl.pallas_call(
+    results = (
+        jax.ShapeDtypeStruct(field, F32),
+        jax.ShapeDtypeStruct((8, 32, 256), F32),
+        jax.ShapeDtypeStruct((8, 32, 256), F32),
+    )
+    made = pl.pallas_call(
         kernel,
-        out_shape=(
-            jax.ShapeDtypeStruct(field, F32),
-            jax.ShapeDtypeStruct((8, 32, 256), F32),
-            jax.ShapeDtypeStruct((8, 32, 256), F32),
-        ),
+        out_shape=results,
         in_specs=[any_] * 8 + [smem] * 3 + [vmem] * 3,
         out_specs=(any_, any_, any_),
         scratch_shapes=[
@@ -632,11 +666,14 @@
             pltpu.VMEM((14, 128, 256), F32),
             pltpu.VMEM(field, F32),
             pltpu.VMEM((13, 128, 256), F32),
-            pltpu.VMEM((12, 136, 256), F32),
+            pltpu.VMEM((12, 128, 256), F32),
+            pltpu.VMEM((12, 128, 256), F32),
+            pltpu.VMEM((12, 128, 256), F32),
             pltpu.VMEM((12, 128, 256), F32),
             pltpu.VMEM((12, 128, 256), F32),
             pltpu.VMEM((14, 128, 128), F32),
             pltpu.VMEM((4, 14, 128, 128), F32),
+            pltpu.VMEM((128, 128), F32),
             pltpu.VMEM((128, 256), F32),
             pltpu.VMEM(field, F32),
             pltpu.VMEM(field, F32),
@@ -654,7 +691,6 @@
             pltpu.VMEM((2, 8, 128), F32),
             pltpu.VMEM((4, 128, 128), I32),
             pltpu.VMEM((8, 4, 8, 256), I32),
-            pltpu.VMEM((128, 128), I32),
             pltpu.VMEM((128, 128), I32),
             pltpu.VMEM((6, 16, 8, 256), I32),
             pltpu.VMEM((2, 2, 128, 256), jnp.int16),
@@ -683,9 +719,17 @@
         ),
         name="flow_gradient",
     )(
-        state_before[0], state_now[0], base_model, buoyancy, latent[0], flow_gain, flow_bias, records, source_wavelet,
+        state_before[0], state_now[0], base_model, buoyancy, latent[0], flow_gain, flow_bias, records, source_wavelet.T,
         source_cell, shot, receiver_depth, jnp.asarray(pick, jnp.bfloat16), jnp.asarray(shift),
     )
+    img, gg, bg = pl.pallas_call(
+        hand_out,
+        out_shape=results,
+        in_specs=[any_] * 3,
+        out_specs=(any_,) * 3,
+        scratch_shapes=[pltpu.VMEM(r.shape, F32) for r in results] + [pltpu.SemaphoreType.DMA((2, 10))],
+        name="hand_out",
+    )(*made)
     return img[None], gg, bg
 
 

time: 72.2 us -> 62.1 us (0.86)
  local copies, waits for them, and re-layouts: 5.44 us -> 0 us
  Pallas kernels: 64.6 us -> 60.6 us
    unnamed x10 -> x0, local copies, waits for them, and re-layouts: 5.44 us -> none
    pallas_call x1 -> x2, Pallas kernels: 64.6 us -> 60.6 us  [the longest x1 58.3 us: shards(): pl.pallas_call(kernel, out_shape=results, in_specs=[any_] * 8 + [smem] *...]
where the time goes in v4:
time: 62.1 us; the launch traced here: 61.9 us
  Pallas kernels  60.6 us (98%)
  between operations  1.29 us (2%)
    pallas_call x1, Pallas kernels, shards(): pl.pallas_call(kernel, out_shape=results, in_specs=[any_] * 8 + [smem] *...  58.3 us
    pallas_call x1, Pallas kernels, shards(): pl.pallas_call(hand_out, out_shape=results, in_specs=[any_] * 3, out_spec...  2.33 us

profile of v4, /device:TPU:1, one launch (start us, length us, event | category | flops | bytes accessed | tf_op | source)
XLA Modules:
  0.0 61.9 jit_solution(3966285732319637921)
XLA Ops:
  1.3 58.3 %flow_gradient.1 = (f32[8,128,256]{2,1,0:T(8,128)}, f32[8,32,256]{2,1,0:T(8,128)}, f32[8,32,256]{2,1,0:T(8,128)}) custom-call(f32[8,128,256]{2,1,0:T(8,128)} %bitcast.5, f32[8,128,256]{2,1,0:T(8,128)} %bitcast.6, f32[8,128,256]{2,1,0:T(8,128)} %base_h.1, f32[8,128,256]{2,1,0:T(8,128)} %buoy_h.1, f32[8,128,256]{2,1,0:T(8,128)} %bitcast.7, ...), custom_call_target="tpu_custom_call" | custom-call | tf_op jit(solution)/shard_map/flow_gradient/pallas_call | solution.py:651
  59.6 2.3 %hand_out.1 = (f32[8,128,256]{2,1,0:T(8,128)}, f32[8,32,256]{2,1,0:T(8,128)}, f32[8,32,256]{2,1,0:T(8,128)}) custom-call(f32[8,128,256]{2,1,0:T(8,128)} %get-tuple-element.9.img, f32[8,32,256]{2,1,0:T(8,128)} %get-tuple-element.10.gg, f32[8,32,256]{2,1,0:T(8,128)} %get-tuple-element.11.bg), custom_call_target="tpu_custom_call" | custom-call | tf_op jit(solution)/shard_map/hand_out/pallas_call | solution.py:725

commit v5 on v4

--- a/solution.py
+++ b/solution.py
@@ -70,7 +70,7 @@
     img_h, gg_h, bg_h,
     U, B, SB, BASE, LAT, PG, RQ, LU, AA, M, Q, CX, CYP, CYM, CZP, CZM, DG, DB, RB, KEY, HIT, IMG, CA, CB, GA, GB, CG, RA, RBUF,
     RX, RY, RZ, RALL, DS, DH, IDX, INV, SIDX, INVH, SE, RE, SG, RG, KT, SR, RR,
-    lsem, es, er, hs, hr, ps, pr, gs, gr, rs, rr, ds_, dr_,
+    lsem, osem, es, er, hs, hr, ps, pr, gs, gr, rs, rr, ds_, dr_,
 ):
     d = lax.axis_index("dom")
     s = lax.axis_index("smp")
@@ -178,13 +178,14 @@
     d_r = rcopy(DS, DH.at[0], ds_.at[1], dr_.at[1], right)
     d_l.start()
     d_r.start()
-    p_z = rcopy(PG.at[s], PG.at[s], ps.at[0], pr.at[0], zlo)
-    p_c = rcopy(PG.at[s], PG.at[s], ps.at[1], pr.at[1], core)
+    p_z = [rcopy(PG.at[s, f], PG.at[s, f], ps.at[0, f], pr.at[0, f], zlo) for f in range(2)]
+    p_c = rcopy(PG.at[s], PG.at[s], ps.at[1, 0], pr.at[1, 0], core)
+    p_z[0].start()
+    p_z[1].start()
     e_l = rcopy(SE.at[0], RE.at[1], es.at[0], er.at[0], left)
     e_r = rcopy(SE.at[1], RE.at[0], es.at[1], er.at[1], right)
     e_l.start()
     e_r.start()
-    p_z.start()
     p_c.start()
 
     ld_r.wait()
@@ -348,10 +349,11 @@
 
     loop(4, invert)
 
-    p_z.wait_recv()
     other = 2 * (1 - zl) + c
-    p_f = rcopy(PG.at[other], PG.at[other], ps.at[2], pr.at[2], core)
-    p_f.start()
+    p_f = [rcopy(PG.at[other, f], PG.at[other, f], ps.at[2, f], pr.at[2, f], core) for f in range(2)]
+    for f in range(2):
+        p_z[f].wait_recv()
+        p_f[f].start()
 
     for cp in r_x:
         cp.wait()
@@ -385,8 +387,9 @@
     ld_lat.wait()
     ld_sb.wait()
     p_c.wait()
-    p_f.wait()
-    p_z.wait_send()
+    for f in range(2):
+        p_f[f].wait()
+        p_z[f].wait_send()
 
     first = d * 8
 
@@ -566,58 +569,85 @@
         return 0
 
     lax.fori_loop(0, 2, outside_back, 0)
-    planes(6, lambda i, y: finish(i + 2 * (i // 3), y))
+
+    pair = 2 * (1 - zl) + c
+
+    def core_copy(i, q):
+        return rcopy(CG.at[2 * i + (1 - c), q], RA.at[i, q], gs.at[i, q], gr.at[i, q], core)
+
+    def zlo_copy(q):
+        return rcopy(CG.at[pair, q], RBUF.at[q], gs.at[2, q], gr.at[2, q], zlo)
+
+    def compact_grads(q):
+        def body(t):
+            k, u = (s + 1 + t // 4) % 4, t % 4
+            at = rows_at(32 * k + T * u)
+            i = IDX[q, at]
+            low, i = i < 128, i & 127
+            for f, src in enumerate((CA, CB)):
+                halves = []
+                for x in range(2):
+                    v = src[2 * q + x, at]
+                    halves.append(jnp.where(low, take(v[:, :128], i), take(v[:, 128:], i)))
+                CG[k, q, f, u] = jnp.where(lane1 < 64, halves[0], halves[1])
+
+        loop(12, body, 4)
+
+    def pass_on(q):
+        core_copy(1 - zl, q).wait()
+        for f in range(2):
+            CG[pair, q, f] = CG[pair, q, f] + RA[1 - zl, q, f]
+        zlo_copy(q).start()
+
+    def begins(i):
+        return 2 + 3 * i - 8 * (i // 2) + 3 * (i // 3)
+
+    def stage(i):
+        loop(1 + i // 2, lambda j: finish(begins(i) + j, 0))
+        q = begins(i) // 2
+        compact_grads(q)
+        core_copy(1 - zl, q).start()
+        core_copy(zl, q).start()
+
+        @pl.when(i >= 1)
+        def _():
+            pass_on(begins(i - 1) // 2)
+
+    loop(4, stage)
     out_i = load(0, IMG, img_h)
-
-    def compact_grads(k):
-        def body(t):
-            at = rows_at(32 * k + T * t)
-            for q in range(4):
-                i = IDX[q, at]
-                low, i = i < 128, i & 127
-                for f, src in enumerate((CA, CB)):
-                    halves = []
-                    for x in (2 * q, 2 * q + 1):
-                        v = src[x, at]
-                        halves.append(jnp.where(low, take(v[:, :128], i), take(v[:, 128:], i)))
-                    CG[k, f, q, t] = jnp.where(lane1 < 64, halves[0], halves[1])
-
-        loop(4, body)
-
-    g_c = []
-    for i in (1 - zl, zl):
-        compact_grads(2 * i + (1 - c))
-        cp = rcopy(CG.at[2 * i + (1 - c)], RA.at[i], gs.at[i], gr.at[i], core)
-        cp.start()
-        g_c.append(cp)
-    pair = 2 * (1 - zl) + c
-    compact_grads(pair)
-    g_c[0].wait()
-    for f in range(2):
-        for q in range(4):
-            CG[pair, f, q] = CG[pair, f, q] + RA[1 - zl, f, q]
-    g_z = rcopy(CG.at[pair], RBUF, gs.at[2], gr.at[2], zlo)
-    g_z.start()
-    g_c[1].wait()
-    g_z.wait()
-
-    def spread(t):
-        at, to = rows_at(32 * s + T * t), rows_at(T * t)
-        for q in range(4):
+    pass_on(3)
+
+    def out_copies(q):
+        at = pl.ds(2 * q, 2)
+        return [
+            pltpu.make_async_copy(GA.at[at], gg_h.at[at], osem.at[0, q]),
+            pltpu.make_async_copy(GB.at[at], bg_h.at[at], osem.at[1, q]),
+        ]
+
+    def last(i):
+        q = begins(i) // 2
+        core_copy(zl, q).wait()
+        zlo_copy(q).wait()
+
+        def spread(t):
+            at, to = rows_at(32 * s + T * t), rows_at(T * t)
             for f, src, out in ((0, CA, GA), (1, CB, GB)):
-                v = RA[zl, f, q, t] + RBUF[f, q, t]
-                for x in (2 * q, 2 * q + 1):
-                    i = INV[x, t]
+                v = RA[zl, q, f, t] + RBUF[q, f, t]
+                for x in range(2):
+                    i = INV[2 * q + x, t]
                     have, i = i >= 0, i & 127
                     g = jnp.concatenate([take(v, i[:, :128]), take(v, i[:, 128:])], axis=1)
-                    out[x, to] = src[x, at] + jnp.where(have, g, 0.0)
-
-    loop(4, spread)
-    out_g = load(1, GA, gg_h)
-    out_b = load(2, GB, bg_h)
+                    out[2 * q + x, to] = src[2 * q + x, at] + jnp.where(have, g, 0.0)
+
+        loop(4, spread, 2)
+        for cp in out_copies(q):
+            cp.start()
+
+    loop(4, last)
     out_i.wait()
-    out_g.wait()
-    out_b.wait()
+    for q in range(4):
+        for cp in out_copies(q):
+            cp.wait()
 
 
 def hand_out(img, gg, bg, img_o, gg_o, bg_o, vi, vg, vb, sem):
@@ -680,9 +710,9 @@
             pltpu.VMEM(field, F32),
             pltpu.VMEM((8, 32, 256), F32),
             pltpu.VMEM((8, 32, 256), F32),
-            pltpu.VMEM((4, 2, 4, 4, 8, 128), F32),
-            pltpu.VMEM((2, 2, 4, 4, 8, 128), F32),
-            pltpu.VMEM((2, 4, 4, 8, 128), F32),
+            pltpu.VMEM((4, 4, 2, 4, 8, 128), F32),
+            pltpu.VMEM((2, 4, 2, 4, 8, 128), F32),
+            pltpu.VMEM((4, 2, 4, 8, 128), F32),
             pltpu.VMEM((7, 64, 128), F32),
             pltpu.VMEM((7, 16, 128), F32),
             pltpu.VMEM((3, 8, 128), F32),
@@ -701,14 +731,15 @@
             pltpu.VMEM((2, 8, 128), F32),
             pltpu.VMEM((2, 8, 128), F32),
             pltpu.SemaphoreType.DMA((8,)),
+            pltpu.SemaphoreType.DMA((2, 4)),
             pltpu.SemaphoreType.DMA((2,)),
             pltpu.SemaphoreType.DMA((2,)),
             pltpu.SemaphoreType.DMA((3, 2)),
             pltpu.SemaphoreType.DMA((3, 2)),
-            pltpu.SemaphoreType.DMA((3,)),
-            pltpu.SemaphoreType.DMA((3,)),
-            pltpu.SemaphoreType.DMA((3,)),
-            pltpu.SemaphoreType.DMA((3,)),
+            pltpu.SemaphoreType.DMA((3, 2)),
+            pltpu.SemaphoreType.DMA((3, 2)),
+            pltpu.SemaphoreType.DMA((3, 4)),
+            pltpu.SemaphoreType.DMA((3, 4)),
             pltpu.SemaphoreType.DMA((10,)),
             pltpu.SemaphoreType.DMA((10,)),
             pltpu.SemaphoreType.DMA((4,)),

time: 62.1 us -> 60.2 us (0.969)
  Pallas kernels: 60.6 us -> 58.8 us
    pallas_call x1, Pallas kernels: 58.3 us -> 56.4 us  [shards(): pl.pallas_call(kernel, out_shape=results, in_specs=[any_] * 8 + [smem] *...]
where the time goes in v5:
time: 60.2 us; the launch traced here: 60.1 us
  Pallas kernels  58.8 us (98%)
  between operations  1.29 us (2%)
    pallas_call x1, Pallas kernels, shards(): pl.pallas_call(kernel, out_shape=results, in_specs=[any_] * 8 + [smem] *...  56.4 us
    pallas_call x1, Pallas kernels, shards(): pl.pallas_call(hand_out, out_shape=results, in_specs=[any_] * 3, out_spec...  2.33 us

profile of v5, /device:TPU:1, one launch (start us, length us, event | category | flops | bytes accessed | tf_op | source)
XLA Modules:
  0.0 60.1 jit_solution(17676698525389047759)
XLA Ops:
  1.3 56.4 %flow_gradient.1 = (f32[8,128,256]{2,1,0:T(8,128)}, f32[8,32,256]{2,1,0:T(8,128)}, f32[8,32,256]{2,1,0:T(8,128)}) custom-call(f32[8,128,256]{2,1,0:T(8,128)} %bitcast.5, f32[8,128,256]{2,1,0:T(8,128)} %bitcast.6, f32[8,128,256]{2,1,0:T(8,128)} %base_h.1, f32[8,128,256]{2,1,0:T(8,128)} %buoy_h.1, f32[8,128,256]{2,1,0:T(8,128)} %bitcast.7, ...), custom_call_target="tpu_custom_call" | custom-call | tf_op jit(solution)/shard_map/flow_gradient/pallas_call | solution.py:681
  57.7 2.3 %hand_out.1 = (f32[8,128,256]{2,1,0:T(8,128)}, f32[8,32,256]{2,1,0:T(8,128)}, f32[8,32,256]{2,1,0:T(8,128)}) custom-call(f32[8,128,256]{2,1,0:T(8,128)} %get-tuple-element.9.img, f32[8,32,256]{2,1,0:T(8,128)} %get-tuple-element.10.gg, f32[8,32,256]{2,1,0:T(8,128)} %get-tuple-element.11.bg), custom_call_target="tpu_custom_call" | custom-call | tf_op jit(solution)/shard_map/hand_out/pallas_call | solution.py:756

commit v6 on v5

--- a/solution.py
+++ b/solution.py
@@ -238,6 +238,23 @@
             LU[0, p + 3, sl] = t
 
     planes(6, lambda i, y: first_lap(i + 1, y))
+
+    def model(k):
+        def body(p):
+            for i in range(2):
+                sl, o = rows_at(32 * k + 16 * i, 16), slice(16 * i, 16 * i + 16)
+                sq = jnp.tanh(LAT[p, sl] * PG[k, 0, p, o].astype(F32) + PG[k, 1, p, o].astype(F32))
+                m = BASE[p, sl] * jnp.exp(0.25 * sq)
+                M[p + 3, sl] = m
+                Q[p, sl] = m * 0.25 * (1.0 - sq * sq)
+
+        loop(8, body, 2)
+
+    ld_base.wait()
+    ld_lat.wait()
+    model(s)
+    p_c.wait()
+    model(2 * zl + (1 - c))
 
     d_l.wait()
     d_r.wait()
@@ -383,13 +400,12 @@
     at_ends(no_edge)
     planes(2, lambda i, y: coef(7 * i, y))
     planes(2, lambda i, y: first_lap(7 * i, y))
-    ld_base.wait()
-    ld_lat.wait()
     ld_sb.wait()
-    p_c.wait()
+    model(other)
     for f in range(2):
         p_f[f].wait()
         p_z[f].wait_send()
+    model(2 * (1 - zl) + (1 - c))
 
     first = d * 8
 
@@ -398,16 +414,9 @@
 
     def step_one(p, y):
         factor = pulse(0, p)
-        for i in range(G // 16):
-            sl, at = rows_at(y + 16 * i, 16), rows_at(PAD + y + 16 * i, 16)
-            k, o = i // 2, slice(16 * (i % 2), 16 * (i % 2) + 16)
-            g = PG[k, 0, p, o].astype(F32)
-            b = PG[k, 1, p, o].astype(F32)
-            sq = jnp.tanh(LAT[p, sl] * g + b)
-            m = BASE[p, sl] * jnp.exp(0.25 * sq)
-            M[p + 3, sl] = m
-            Q[p, sl] = m * 0.25 * (1.0 - sq * sq)
-            new = 2.0 * U[0, p + 3, at] - SB[p, sl] + m * LU[0, p + 3, sl]
+        for i in range(16):
+            sl, at = rows_at(y + T * i), rows_at(PAD + y + T * i)
+            new = 2.0 * U[0, p + 3, at] - SB[p, sl] + M[p + 3, sl] * LU[0, p + 3, sl]
             U[1, p + 3, at] = new + factor * HIT[sl]
 
     planes(6, lambda i, y: step_one(i + 2 * (i // 3), y))
@@ -523,7 +532,7 @@
         for sl, at, _, t in laps(2, p, y):
             a2, a3 = AA[1, p + 3, sl], AA[2, p + 3, sl]
             a1 = AA[0, p + 3, sl] + t + 2.0 * a2 - a3
-            img = AA[3, p + 3, sl] * LU[3, p + 3, sl] + a3 * LU[2, p + 3, sl]
+            img = IMG[p, sl] + a3 * LU[2, p + 3, sl]
             img = img + a2 * LU[1, p + 3, sl] + a1 * LU[0, p + 3, sl]
             IMG[p, sl] = img
             com = img * Q[p, sl]
@@ -535,6 +544,7 @@
             sl = rows_at(y + T * i)
             r = U[1, p + 3, rows_at(PAD + y + T * i)] - twice(RB[0, p + 3, sl])
             AA[0, p + 3, sl] = jnp.where(lane_f == twice(DB[p + 3, sl]), r, 0.0)
+            IMG[p, sl] = AA[3, p + 3, sl] * LU[3, p + 3, sl]
 
     planes(8, resid_one)
 

time: 60.2 us -> 60.2 us (level)
  no operation moved by 1% of the time
where the time goes in v6:
time: 60.2 us; the launch traced here: 60 us
  Pallas kernels  58.7 us (98%)
  between operations  1.29 us (2%)
    pallas_call x1, Pallas kernels, shards(): pl.pallas_call(kernel, out_shape=results, in_specs=[any_] * 8 + [smem] *...  56.4 us
    pallas_call x1, Pallas kernels, shards(): pl.pallas_call(hand_out, out_shape=results, in_specs=[any_] * 3, out_spec...  2.33 us

profile of v6, /device:TPU:1, one launch (start us, length us, event | category | flops | bytes accessed | tf_op | source)
XLA Modules:
  0.0 60.0 jit_solution(210040412425621775)
XLA Ops:
  1.3 56.4 %flow_gradient.1 = (f32[8,128,256]{2,1,0:T(8,128)}, f32[8,32,256]{2,1,0:T(8,128)}, f32[8,32,256]{2,1,0:T(8,128)}) custom-call(f32[8,128,256]{2,1,0:T(8,128)} %bitcast.5, f32[8,128,256]{2,1,0:T(8,128)} %bitcast.6, f32[8,128,256]{2,1,0:T(8,128)} %base_h.1, f32[8,128,256]{2,1,0:T(8,128)} %buoy_h.1, f32[8,128,256]{2,1,0:T(8,128)} %bitcast.7, ...), custom_call_target="tpu_custom_call" | custom-call | tf_op jit(solution)/shard_map/flow_gradient/pallas_call | solution.py:691
  57.7 2.3 %hand_out.1 = (f32[8,128,256]{2,1,0:T(8,128)}, f32[8,32,256]{2,1,0:T(8,128)}, f32[8,32,256]{2,1,0:T(8,128)}) custom-call(f32[8,128,256]{2,1,0:T(8,128)} %get-tuple-element.9.img, f32[8,32,256]{2,1,0:T(8,128)} %get-tuple-element.10.gg, f32[8,32,256]{2,1,0:T(8,128)} %get-tuple-element.11.bg), custom_call_target="tpu_custom_call" | custom-call | tf_op jit(solution)/shard_map/hand_out/pallas_call | solution.py:766
